TPU v7x, 32 devices: a whole 2x2x4 slice. The times are simulated.
32 devices in a mesh: frame: 16 (over z, x, core), clip: 2 (over y).
Axes of the slice: x: 2, y: 2, z: 4, core: 2. Of those that a mesh axis runs over, the one named last changes fastest.
Arguments:
- latents: bfloat16 [64, 576, 640], P(('clip', 'frame')), parts along dimension 0, may hold values from -6 to 6
- offsets: int32 [32], P(('clip', 'frame')), parts along dimension 0, may hold values from 0 to 1
- source_device: int32 [2], P('clip'), parts along dimension 0, may hold values from 0 to 15
- reference_bank: bfloat16 [32, 576, 640], P(('clip', 'frame')), parts along dimension 0, may hold values from -6 to 6
- spatial_in: bfloat16 [640, 960], P('frame'), may hold values from -7.1151247 to 7.1151247
- spatial_out: bfloat16 [320, 640], P(None, 'frame'), may hold values from -0.3125 to 0.3125
- temporal_in: bfloat16 [640, 960], P('frame'), may hold values from -7.1151247 to 7.1151247
- temporal_out: bfloat16 [320, 640], P(None, 'frame'), may hold values from -0.3125 to 0.3125
Outputs:
- blended: bfloat16 [64, 576, 640], P(('clip', 'frame')), parts along dimension 0
There are 2 independent parts, one for each index of `clip`. A program takes and returns all parts, laid end to end along the dimension named above; an argument that names none is the same for every part. Nothing has to cross between parts.
All inputs are finite; a program needn't handle non-finite values.
Results may differ from a plain program's by a relative error of at most 0.018.
The roundings to bfloat16 on the way count: a program that leaves them out, or rounds other values in their place, can miss the bound.
Values may be sent and summed in bfloat16 or wider, within the bound.
A program may use at most 128 MiB of HBM per device.

v0:
```python
import jax
import jax.numpy as jnp
from jax import lax
from jax.sharding import PartitionSpec as P

C = 640
HW = 576
HEADS = 4
HEAD_DIM = 80
WIN = 16


def broadcast(block, axis, holder):
    block = jnp.where(lax.axis_index(axis) == holder, block, jnp.zeros_like(block))
    return lax.psum(block, axis)


def shifted(value, axis, steps):
    count = lax.axis_size(axis)
    first, last = (max(0, -steps), min(count, count - steps))
    return lax.ppermute(value, axis, [(source, source + steps) for source in range(first, last)])


def normalize(values):
    values = values.astype(jnp.float32)
    center = values - jnp.mean(values, axis=-1, keepdims=True)
    spread = jnp.mean(center * center, axis=-1, keepdims=True)
    return center * lax.rsqrt(spread + 1e-05)


def softmax_rounded(scores):
    scores = scores - jnp.max(scores, axis=-1, keepdims=True)
    expo = jnp.exp(scores)
    return (expo / jnp.sum(expo, axis=-1, keepdims=True)).astype(jnp.bfloat16)


def attend(queries, keys, values):
    count = queries.shape[0]
    scale = HEAD_DIM ** (-0.5)
    qh = queries.reshape(count, HEADS, HEAD_DIM)
    kh = keys.reshape(keys.shape[0], HEADS, HEAD_DIM)
    vh = values.reshape(values.shape[0], HEADS, HEAD_DIM)
    scores = jnp.einsum("qhd,khd->hqk", qh, kh, preferred_element_type=jnp.float32) * scale
    weights = softmax_rounded(scores)
    result = jnp.einsum("hqk,khd->qhd", weights, vh, preferred_element_type=jnp.float32)
    return result.reshape(count, HEADS * HEAD_DIM).astype(jnp.bfloat16)


def body(
    latents,
    offsets,
    source_device,
    reference_bank,
    spatial_in,
    spatial_out,
    temporal_in,
    temporal_out,
):
    frames_here = latents.shape[0]
    inner = HEADS * HEAD_DIM
    scale = HEAD_DIM ** (-0.5)
    shards = lax.axis_size("frame")
    position = lax.axis_index("frame")
    frames_total = shards * frames_here
    rows = frames_here * HW
    picked = broadcast(reference_bank[0], "frame", source_device[0])
    hidden = normalize(latents).astype(jnp.bfloat16).reshape(rows, C)
    ref_hidden = normalize(picked).astype(jnp.bfloat16)
    stacked = jnp.concatenate([hidden, ref_hidden], axis=0)
    spatial_whole = lax.all_gather(spatial_in, "frame", axis=0, tiled=True)
    proj = jnp.dot(stacked, spatial_whole, preferred_element_type=jnp.float32).astype(jnp.bfloat16)
    ref_keys = proj[rows:, inner : 2 * inner]
    ref_vals = proj[rows:, 2 * inner :]
    outputs = []
    for frame in range(frames_here):
        block = proj[frame * HW : (frame + 1) * HW]
        keys = jnp.concatenate([block[:, inner : 2 * inner], ref_keys], axis=0)
        vals = jnp.concatenate([block[:, 2 * inner :], ref_vals], axis=0)
        outputs.append(attend(block[:, :inner], keys, vals))
    attended = jnp.concatenate(outputs, axis=0)
    mixed = jnp.dot(
        attended,
        lax.all_gather(spatial_out, "frame", axis=1, tiled=True),
        preferred_element_type=jnp.float32,
    )
    first = (latents.astype(jnp.float32).reshape(rows, C) + mixed).astype(jnp.bfloat16)
    hidden_two = normalize(first).astype(jnp.bfloat16)
    temporal_whole = lax.all_gather(temporal_in, "frame", axis=0, tiled=True)
    tproj = jnp.dot(hidden_two, temporal_whole, preferred_element_type=jnp.float32)
    tproj = tproj.astype(jnp.bfloat16).reshape(frames_here, HW, 3 * inner)
    back = WIN // 2 - 1
    left_count = (back + frames_here - 1) // frames_here
    right_count = (WIN // 2 + 1) // frames_here
    keyvals = tproj[:, :, inner:]
    pieces = []
    for step in range(-left_count, right_count + 1):
        if step == 0:
            pieces.append(keyvals)
        else:
            pieces.append(shifted(keyvals, "frame", -step))
    nearby = jnp.concatenate(pieces, axis=0)
    start = left_count * frames_here - back + offsets[0]
    window = lax.dynamic_slice_in_dim(nearby, start, WIN, 0)
    global_frame = (position - left_count) * frames_here + start + jnp.arange(WIN, dtype=jnp.int32)
    valid = (global_frame >= 0) & (global_frame < frames_total)
    queries = tproj[:, :, :inner].reshape(frames_here, HW, HEADS, HEAD_DIM)
    wkeys = window[:, :, :inner].reshape(WIN, HW, HEADS, HEAD_DIM)
    wvals = window[:, :, inner:].reshape(WIN, HW, HEADS, HEAD_DIM)
    scores = (
        jnp.einsum("fthd,wthd->thfw", queries, wkeys, preferred_element_type=jnp.float32) * scale
    )
    scores = jnp.where(valid[None, None, None, :], scores, -1e30)
    weights = softmax_rounded(scores)
    result = jnp.einsum("thfw,wthd->fthd", weights, wvals, preferred_element_type=jnp.float32)
    tattended = result.reshape(rows, inner).astype(jnp.bfloat16)
    second = jnp.dot(
        tattended,
        lax.all_gather(temporal_out, "frame", axis=1, tiled=True),
        preferred_element_type=jnp.float32,
    )
    blended = (first.astype(jnp.float32) + second).astype(jnp.bfloat16)
    return blended.reshape(frames_here, HW, C)


def solution(mesh):
    placed = (
        P(("clip", "frame"), None, None),
        P(("clip", "frame")),
        P("clip"),
        P(("clip", "frame"), None, None),
        P("frame", None),
        P(None, "frame"),
        P("frame", None),
        P(None, "frame"),
    )
    return jax.shard_map(
        body,
        mesh=mesh,
        in_specs=placed,
        out_specs=P(("clip", "frame"), None, None),
        check_vma=False,
    )
```

profile of v0, /device:TPU:0, one launch (start us, length us, event | category | flops | bytes accessed | tf_op | source)
XLA Modules:
  0.0 469.2 jit_solution(4526484842629627030)
XLA Ops:
  11.2 25.6 %all_gather.13 = bf16[320,640]{0,1:T(8,128)(2,1)S(1)} all-gather(bf16[320,40]{0,1:T(8,128)(2,1)S(1)} %copy-done.3), channel_id=1, replica_groups=mesh['frame'=16,'clip'=2] {'frame'}, dimensions={1}, use_global_device_ids=true | all-gather | bytes 435200 | tf_op jit(solution)/shard_map/all_gather | solution.py:83
  36.8 68.0 %all-reduce.2.cloned.1.call-done = bf16[576,640]{1,0:T(8,128)(2,1)} async-done(((bf16[576,640]{1,0:T(8,128)(2,1)}), bf16[576,640]{1,0:T(8,128)(2,1)}) %all-reduce.2.cloned.1.call-update) | async-done | bytes 737296 | tf_op jit(solution)/shard_map/psum | solution.py:15
  107.6 2.3 fusion.25
  109.9 36.7 %all-gather.3.cloned.1.call-done = bf16[640,960]{1,0:T(8,128)(2,1)} async-done(((bf16[40,960]{1,0:T(8,128)(2,1)}), bf16[640,960]{1,0:T(8,128)(2,1)}) %all-gather.3.cloned.1.call-update) | async-done | bytes 1228816 | tf_op jit(solution)/shard_map/all_gather | solution.py:70
  146.6 4.4 convolution_convert_fusion.1
  154.4 8.6 %fusion.47 = (f32[4,576]{1,0:T(4,128)S(1)}, f32[4,576,1152]{2,1,0:T(8,128)}) fusion(bf16[576,4,80]{0,2,1:T(8,128)(2,1)} %bitcast.61, bf16[1152,4,80]{0,2,1:T(8,128)(2,1)} %bitcast.59), kind=kOutput, calls=%fused_computation.82 | convolution fusion | flops 432637056 | bytes 11731968 | tf_op jit(solution)/shard_map/sub | solution.py:32
  163.0 8.3 %fusion.46 = (f32[4,576]{1,0:T(4,128)S(1)}, f32[4,576,1152]{2,1,0:T(8,128)}) fusion(bf16[576,4,80]{0,2,1:T(8,128)(2,1)} %bitcast.60, bf16[1152,4,80]{0,2,1:T(8,128)(2,1)S(1)} %bitcast.57), kind=kOutput, calls=%fused_computation.81 | convolution fusion | flops 432637056 | bytes 11731968 | tf_op jit(solution)/shard_map/sub | solution.py:32
  171.3 6.2 %fusion.31 = bf16[4,80,576]{2,1,0:T(8,128)(2,1)S(1)} fusion(bf16[1152,4,80]{0,2,1:T(8,128)(2,1)} %bitcast.58, f32[4,576,1152]{2,1,0:T(8,128)} %get-tuple-element.18, f32[4,576]{1,0:T(4,128)S(1)} %get-tuple-element.17), kind=kOutput, calls=%fused_computation.47 | convolution fusion | flops 430166016 | bytes 11731968 | tf_op jit(solution)/shard_map/hqk,khd->qhd/dot_general | solution.py:45
  178.8 2.1 fusion.30
  182.9 3.9 all-gather.5.cloned.1.call-done
  186.8 5.0 %convolution_convert_fusion = bf16[1152,960]{0,1:T(8,128)(2,1)} fusion(bf16[640,960]{1,0:T(8,128)(2,1)} %all-gather.5.cloned.1.call-done, bf16[1152,640]{1,0:T(8,128)(2,1)S(1)} %get-tuple-element.20, f32[1152]{0:T(1024)S(1)} %add_rsqrt_fusion, f32[1152]{0:T(1024)S(1)} %broadcast_multiply_fusion), kind=kOutput, calls=%fused_computation.19 | convolution fusion | flops 1419632640 | bytes 4924416 | tf_op jit(solution)/shard_map/dot_general | solution.py:89
  191.8 2.8 copy.9
  194.6 1.8 slice.58
  196.5 3.6 collective-permute-start
  200.0 3.3 collective-permute-start.1
  203.3 3.4 collective-permute-start.2
  206.7 2.4 collective-permute-start.3
  210.4 21.4 %collective-permute-done = bf16[2,576,640]{2,1,0:T(8,128)(2,1)} collective-permute-done((bf16[2,576,640]{2,1,0:T(8,128)(2,1)}, bf16[2,576,640]{2,1,0:T(8,128)(2,1)}, u32[]{:S(2)}, u32[]{:S(2)}) %collective-permute-start) | collective-permute-done | bytes 1474592 | tf_op jit(solution)/shard_map/ppermute | solution.py:21
  233.1 63.9 %collective-permute-done.1 = bf16[2,576,640]{2,1,0:T(8,128)(2,1)} collective-permute-done((bf16[2,576,640]{2,1,0:T(8,128)(2,1)}, bf16[2,576,640]{2,1,0:T(8,128)(2,1)}, u32[]{:S(2)}, u32[]{:S(2)}) %collective-permute-start.1) | collective-permute-done | bytes 1474592 | tf_op jit(solution)/shard_map/ppermute | solution.py:21
  298.3 30.3 %collective-permute-done.2 = bf16[2,576,640]{2,1,0:T(8,128)(2,1)} collective-permute-done((bf16[2,576,640]{2,1,0:T(8,128)(2,1)}, bf16[2,576,640]{2,1,0:T(8,128)(2,1)}, u32[]{:S(2)}, u32[]{:S(2)}) %collective-permute-start.2) | collective-permute-done | bytes 1474592 | tf_op jit(solution)/shard_map/ppermute | solution.py:21
  329.9 35.5 %all_gather.15 = bf16[320,640]{0,1:T(8,128)(2,1)} all-gather(bf16[320,40]{0,1:T(8,128)(2,1)S(1)} %copy-done.4), channel_id=1, replica_groups=mesh['frame'=16,'clip'=2] {'frame'}, dimensions={1}, use_global_device_ids=true | all-gather | bytes 435200 | tf_op jit(solution)/shard_map/all_gather | solution.py:118
  367.5 3.0 copy.13
  372.0 1.6 constant_dynamic-update-slice_fusion.7
  384.2 6.9 %constant_dynamic-slice_fusion.1 = (bf16[16,576,320]{2,1,0:T(8,128)(2,1)}, bf16[16,576,320]{2,1,0:T(8,128)(2,1)}) fusion(bf16[18,576,640]{2,1,0:T(8,128)(2,1)S(1)} %constant_dynamic-update-slice_fusion, s32[]{:T(128)S(6)} %select_n.21, s32[]{:T(128)S(6)} %add.76), kind=kLoop, calls=%fused_computation.74 | loop fusion | bytes 23592968 | tf_op jit(solution)/shard_map/slice | solution.py:107
  391.2 9.8 %copy.12 = bf16[16,576,320]{1,2,0:T(8,128)(2,1)} copy(bf16[16,576,320]{2,1,0:T(8,128)(2,1)} %get-tuple-element.5) | data formatting | bytes 11796480 | tf_op jit(solution)/shard_map/slice | solution.py:107
  401.0 15.0 %copy.14 = bf16[16,576,4,80]{3,0,2,1:T(8,128)(2,1)} copy(bf16[16,576,4,80]{1,3,2,0:T(8,128)(2,1)} %bitcast.48) | data formatting | bytes 11796480 | tf_op jit(solution)/shard_map/reshape | solution.py:107
  416.0 9.8 %copy.10 = bf16[16,576,320]{1,2,0:T(8,128)(2,1)} copy(bf16[16,576,320]{2,1,0:T(8,128)(2,1)} %get-tuple-element.6) | data formatting | bytes 11796480 | tf_op jit(solution)/shard_map/slice | solution.py:108
  425.8 14.9 %copy.15 = bf16[16,576,4,80]{3,0,2,1:T(8,128)(2,1)} copy(bf16[16,576,4,80]{1,3,2,0:T(8,128)(2,1)} %bitcast.49) | data formatting | bytes 11796480 | tf_op jit(solution)/shard_map/reshape | solution.py:108
  440.7 9.2 %fusion.48 = (f32[576,4,2]{2,1,0:T(4,128)S(1)}, f32[576,4,2,16]{3,2,1,0:T(2,128)}) fusion(pred[16]{0:T(512)(128)(4,1)S(1)} %compare_and_fusion, bf16[2,576,4,80]{3,0,2,1:T(2,128)(2,1)S(1)} %copy.13, bf16[16,576,4,80]{3,0,2,1:T(8,128)(2,1)} %copy.14), kind=kOutput, calls=%fused_computation.83 | convolution fusion | flops 12091407 | bytes 6948880 | tf_op jit(solution)/shard_map/sub | solution.py:32
  449.9 6.1 %fusion.29 = bf16[2,576,4,80]{3,0,2,1:T(2,128)(2,1)S(1)} fusion(bf16[16,576,4,80]{3,0,2,1:T(8,128)(2,1)} %copy.15, f32[576,4,2,16]{3,2,1,0:T(2,128)} %get-tuple-element.22, f32[576,4,2]{2,1,0:T(4,128)S(1)} %get-tuple-element.21), kind=kOutput, calls=%fused_computation.45 | convolution fusion | flops 12312576 | bytes 6948864 | tf_op jit(solution)/shard_map/thfw,wthd->fthd/dot_general | solution.py:114
  456.1 2.8 copy.16
  459.5 3.2 fusion.16
  (56 shorter events, 32.3 us)
Async XLA Ops:
  6.5 3.2 copy-start
  6.5 98.3 %all-reduce.2.cloned.1.call-start = ((), (), s32[]{:S(2)}) async-start(), calls=%async_computation | async-start | bytes 1474560 | tf_op jit(solution)/shard_map/psum | solution.py:15
  8.3 138.3 %all-gather.3.cloned.1.call-start = ((), (), s32[]{:S(2)}) async-start(), calls=%async_computation.1 | async-start | bytes 1392640 | tf_op jit(solution)/shard_map/all_gather | solution.py:70
  9.0 177.8 %all-gather.5.cloned.1.call-start = ((), (), s32[]{:S(2)}) async-start(), calls=%async_computation.2 | async-start | bytes 1392640 | tf_op jit(solution)/shard_map/all_gather | solution.py:88
  9.8 1.4 copy-start.3
  171.3 7.5 %copy-start.5 = (f32[4,576,1152]{2,1,0:T(8,128)S(1)}, f32[4,576,1152]{2,1,0:T(8,128)}, u32[]{:S(2)}) copy-start(f32[4,576,1152]{2,1,0:T(8,128)} %get-tuple-element.16) | copy-start | bytes 31850500
  182.3 4.6 copy-start.1
  191.8 138.1 %copy-start.4 = (bf16[320,40]{0,1:T(8,128)(2,1)S(1)}, bf16[320,40]{0,1:T(8,128)(2,1)}, u32[]{:S(2)}) copy-start(bf16[320,40]{0,1:T(8,128)(2,1)} %param.15) | copy-start | bytes 76804
  196.5 35.4 %collective-permute-start = (bf16[2,576,640]{2,1,0:T(8,128)(2,1)}, bf16[2,576,640]{2,1,0:T(8,128)(2,1)}, u32[]{:S(2)}, u32[]{:S(2)}) collective-permute-start(bf16[2,576,640]{2,1,0:T(8,128)(2,1)} %slice.58), channel_id=1, source_target_pairs={{0,8},{2,10},{4,12},{6,14},{8,16},{10,18},{12,20},{14,22},{16,24},... | collective-permute-start | bytes 4423688 | tf_op jit(solution)/shard_map/ppermute | solution.py:21
  200.0 97.0 %collective-permute-start.1 = (bf16[2,576,640]{2,1,0:T(8,128)(2,1)}, bf16[2,576,640]{2,1,0:T(8,128)(2,1)}, u32[]{:S(2)}, u32[]{:S(2)}) collective-permute-start(bf16[2,576,640]{2,1,0:T(8,128)(2,1)} %slice.58), channel_id=1, source_target_pairs={{0,6},{2,8},{4,10},{6,12},{8,14},{10,16},{12,18},{14,20},{16,22},{... | collective-permute-start | bytes 4423688 | tf_op jit(solution)/shard_map/ppermute | solution.py:21
  203.3 125.3 %collective-permute-start.2 = (bf16[2,576,640]{2,1,0:T(8,128)(2,1)}, bf16[2,576,640]{2,1,0:T(8,128)(2,1)}, u32[]{:S(2)}, u32[]{:S(2)}) collective-permute-start(bf16[2,576,640]{2,1,0:T(8,128)(2,1)} %slice.58), channel_id=1, source_target_pairs={{0,4},{2,6},{4,8},{6,10},{8,12},{10,14},{12,16},{14,18},{16,20},{1... | collective-permute-start | bytes 4423688 | tf_op jit(solution)/shard_map/ppermute | solution.py:21
  206.7 168.6 %collective-permute-start.3 = (bf16[2,576,640]{2,1,0:T(8,128)(2,1)}, bf16[2,576,640]{2,1,0:T(8,128)(2,1)}, u32[]{:S(2)}, u32[]{:S(2)}) collective-permute-start(bf16[2,576,640]{2,1,0:T(8,128)(2,1)} %slice.58), channel_id=1, source_target_pairs={{0,2},{2,4},{4,6},{6,8},{8,10},{10,12},{12,14},{14,16},{16,18},{18... | collective-permute-start | bytes 4423688 | tf_op jit(solution)/shard_map/ppermute | solution.py:21
  209.1 168.6 %collective-permute-start.4 = (bf16[2,576,640]{2,1,0:T(8,128)(2,1)}, bf16[2,576,640]{2,1,0:T(8,128)(2,1)}, u32[]{:S(2)}, u32[]{:S(2)}) collective-permute-start(bf16[2,576,640]{2,1,0:T(8,128)(2,1)} %slice.58), channel_id=1, source_target_pairs={{2,0},{4,2},{6,4},{8,6},{10,8},{12,10},{14,12},{16,14},{18,16},{20... | collective-permute-start | bytes 4423688 | tf_op jit(solution)/shard_map/ppermute | solution.py:21
  231.8 147.5 %collective-permute-start.5 = (bf16[2,576,640]{2,1,0:T(8,128)(2,1)}, bf16[2,576,640]{2,1,0:T(8,128)(2,1)}, u32[]{:S(2)}, u32[]{:S(2)}) collective-permute-start(bf16[2,576,640]{2,1,0:T(8,128)(2,1)} %slice.58), channel_id=1, source_target_pairs={{4,0},{6,2},{8,4},{10,6},{12,8},{14,10},{16,12},{18,14},{20,16},{2... | collective-permute-start | bytes 4423688 | tf_op jit(solution)/shard_map/ppermute | solution.py:21
  297.0 84.0 %collective-permute-start.6 = (bf16[2,576,640]{2,1,0:T(8,128)(2,1)}, bf16[2,576,640]{2,1,0:T(8,128)(2,1)}, u32[]{:S(2)}, u32[]{:S(2)}) collective-permute-start(bf16[2,576,640]{2,1,0:T(8,128)(2,1)} %slice.58), channel_id=1, source_target_pairs={{6,0},{8,2},{10,4},{12,6},{14,8},{16,10},{18,12},{20,14},{22,16},{... | collective-permute-start | bytes 4423688 | tf_op jit(solution)/shard_map/ppermute | solution.py:21
  328.6 54.0 %collective-permute-start.7 = (bf16[2,576,640]{2,1,0:T(8,128)(2,1)}, bf16[2,576,640]{2,1,0:T(8,128)(2,1)}, u32[]{:S(2)}, u32[]{:S(2)}) collective-permute-start(bf16[2,576,640]{2,1,0:T(8,128)(2,1)} %slice.58), channel_id=1, source_target_pairs={{8,0},{10,2},{12,4},{14,6},{16,8},{18,10},{20,12},{22,14},{24,16},... | collective-permute-start | bytes 4423688 | tf_op jit(solution)/shard_map/ppermute | solution.py:21
  456.1 3.4 copy-start.2
Sparse Core Ops, SparseCore 0:
  10.8 94.0 all-reduce.1
  107.4 39.1 all-gather.2
  149.1 37.6 all-gather.4
where the time goes:
time: 471 us; the launch traced here: 469 us
  waiting for transfers between devices  226 us (48%)
  local copies, waits for them, and re-layouts  85.7 us (18%)
  blocking collectives  61.1 us (13%)
  matrix products  54.6 us (12%)
  starting transfers between devices  17.9 us (4%)
  between operations  14.8 us (3%)
  other arithmetic  9.55 us (2%)
    ppermute x8, waiting for transfers between devices, shifted(): lax.ppermute(value, axis, [(source, source + steps) for source in range(f...  116 us
    psum x1, waiting for transfers between devices, broadcast(): return lax.psum(block, axis)  68 us
    all_gather x1, waiting for transfers between devices, body(): spatial_whole = lax.all_gather(spatial_in, 'frame', axis=0, tiled=True)  36.7 us
    all_gather x1, blocking collectives, body(): lax.all_gather(temporal_out, 'frame', axis=1, tiled=True)  35.5 us
    sub x3, matrix products, softmax_rounded(): scores = scores - jnp.max(scores, axis=-1, keepdims=True)  26.1 us
    all_gather x1, blocking collectives, body(): lax.all_gather(spatial_out, 'frame', axis=1, tiled=True)  25.6 us
    ppermute x8, starting transfers between devices, shifted(): lax.ppermute(value, axis, [(source, source + steps) for source in range(f...  17.8 us
    slice x2, local copies, waits for them, and re-layouts, body(): wkeys = window[:, :, :inner].reshape(WIN, HW, HEADS, HEAD_DIM)  16.8 us
  transfers between devices with their start and end apart: 11, of which 6 were waited for; matrix products, arithmetic and copies ran while one was open for 12% of the time, Pallas kernels for 0%

commit v1 on v0

v1 whole, which is shorter than its diff:
```python
import functools
import math

import jax
import jax.numpy as jnp
from jax import lax
from jax.experimental import pallas as pl
from jax.experimental.pallas import tpu as pltpu
from jax.sharding import PartitionSpec as P

C = 640
HW = 576
HEADS = 4
HEAD_DIM = 80
INNER = 320
WIDE = 384
WIN = 16
MESH = pl.DeviceIdType.MESH
FACTOR = HEAD_DIM ** (-0.5) * math.log2(math.e)
VMEM_LIMIT = 60 * 1024 * 1024
SPANS = tuple(
    (h * HEAD_DIM // 128, (h * HEAD_DIM + HEAD_DIM - 1) // 128 + 1) for h in range(HEADS)
)


def up16(count):
    return -(-count // 16) * 16


def normalize(values):
    values = values.astype(jnp.float32)
    center = values - jnp.mean(values, axis=-1, keepdims=True)
    spread = jnp.mean(center * center, axis=-1, keepdims=True)
    return center * lax.rsqrt(spread + 1e-05)


def dot(a, b):
    return jnp.dot(a, b, preferred_element_type=jnp.float32)


def dot_t(a, b):
    return lax.dot_general(a, b, (((1,), (1,)), ((), ())), preferred_element_type=jnp.float32)


def remote(src, dst, send, recv, peer):
    return pltpu.make_async_remote_copy(
        src_ref=src, dst_ref=dst, send_sem=send, recv_sem=recv,
        device_id={"frame": peer}, device_id_type=MESH,
    )


def greet(n, me):
    barrier = pltpu.get_barrier_semaphore()
    for k in range(1, n):
        pl.semaphore_signal(
            barrier, inc=1, device_id={"frame": lax.rem(me + k, n)}, device_id_type=MESH
        )
    pl.semaphore_wait(barrier, n - 1)


def exchange_kernel(n, x_ref, o_ref, send, recv, local):
    me = lax.axis_index("frame")
    greet(n, me)
    copies = []
    for k in range(1, n):
        peer = lax.rem(me + k, n)
        copy = remote(x_ref.at[peer], o_ref.at[me], send.at[k], recv.at[k], peer)
        copy.start()
        copies.append(copy)
    own = pltpu.make_async_copy(x_ref.at[me], o_ref.at[me], local)
    own.start()
    own.wait()
    for copy in copies:
        copy.wait()


def exchange(x, ident):
    n = x.shape[0]
    return pl.pallas_call(
        functools.partial(exchange_kernel, n),
        out_shape=jax.ShapeDtypeStruct(x.shape, x.dtype),
        in_specs=[pl.BlockSpec(memory_space=pl.ANY)],
        out_specs=pl.BlockSpec(memory_space=pl.ANY),
        scratch_shapes=[
            pltpu.SemaphoreType.DMA((n,)),
            pltpu.SemaphoreType.DMA((n,)),
            pltpu.SemaphoreType.DMA,
        ],
        compiler_params=pltpu.CompilerParams(collective_id=ident, has_side_effects=True),
    )(x)


def collect_kernel(
    n, rows, holders, src_ref, bank_ref, w_ref, ref_ref, wall_ref,
    got, chunk, bsend, brecv, wsend, wrecv, rsend, rrecv, local,
):
    me = lax.axis_index("frame")
    sub, level = lax.rem(me, 4), me // 4
    levels = n // 4
    xmate = level * 4 + lax.rem(sub + 2, 4)
    cmate = me + 1 - 2 * lax.rem(me, 2)
    greet(n, me)
    for k in range(1, n):
        peer = lax.rem(me + k, n)

        @pl.when(peer < holders)
        def _():
            start = pl.multiple_of(peer * rows, 16)
            remote(
                bank_ref.at[0, pl.ds(start, rows)], got.at[me], bsend.at[k], brecv.at[k], peer
            ).start()

    @pl.when(me < holders)
    def _():
        start = pl.multiple_of(me * rows, 16)
        own = pltpu.make_async_copy(bank_ref.at[0, pl.ds(start, rows)], got.at[me], local.at[0])
        own.start()
        own.wait()

    place = pltpu.make_async_copy(w_ref, wall_ref.at[me], local.at[1])
    place.start()

    def z_copy(k):
        peer = lax.rem(me + 4 * k, n)
        return remote(w_ref, wall_ref.at[me], wsend.at[0, k], wrecv.at[0, k], peer)

    def hop_copy(stage, block, slot, peer):
        part = wall_ref.at[block]
        return remote(part, part, wsend.at[stage, slot], wrecv.at[stage, slot], peer)

    for k in range(1, levels):
        z_copy(k).start()
    place.wait()
    firsts = []
    for k in range(levels):
        block = lax.rem(me + n - 4 * k, n)
        if k:
            z_copy(k).wait_recv()
        copy = hop_copy(1, block, k, xmate)
        copy.start()
        firsts.append(copy)
        last = hop_copy(2, block, k, cmate)
        last.start()
        firsts.append(last)
    for k in range(1, n):
        peer = lax.rem(me + k, n)

        @pl.when(me < holders)
        def _():
            start = pl.multiple_of(me * rows, 16)
            remote(
                bank_ref.at[0, pl.ds(start, rows)], got.at[me], bsend.at[k], brecv.at[k], peer
            ).wait_recv()

        @pl.when(peer < holders)
        def _():
            start = pl.multiple_of(peer * rows, 16)
            remote(
                bank_ref.at[0, pl.ds(start, rows)], got.at[me], bsend.at[k], brecv.at[k], peer
            ).wait_send()

    @pl.when(me < holders)
    def _():
        chunk[...] = got[src_ref[0]]
        for k in range(1, n):
            peer = lax.rem(me + k, n)
            remote(chunk, ref_ref.at[me], rsend.at[k], rrecv.at[k], peer).start()
        own = pltpu.make_async_copy(chunk, ref_ref.at[me], local.at[0])
        own.start()
        own.wait()

    for k in range(levels):
        block = lax.rem(xmate + n - 4 * k, n)
        hop_copy(1, block, k, xmate).wait_recv()
        last = hop_copy(2, block, levels + k, cmate)
        last.start()
        firsts.append(last)
    for k in range(levels):
        for side in range(2):
            origin = cmate if side == 0 else lax.rem(cmate // 4 * 4 + lax.rem(cmate + 2, 4), n)
            block = lax.rem(origin + n - 4 * k, n)
            hop_copy(2, block, side * levels + k, cmate).wait_recv()
    for copy in firsts:
        copy.wait_send()
    for k in range(1, levels):
        z_copy(k).wait_send()
    for k in range(1, n):
        peer = lax.rem(me + k, n)
        sender = lax.rem(me + n - k, n)

        @pl.when(sender < holders)
        def _():
            remote(chunk, ref_ref.at[sender], rsend.at[k], rrecv.at[k], peer).wait_recv()

        @pl.when(me < holders)
        def _():
            remote(chunk, ref_ref.at[me], rsend.at[k], rrecv.at[k], peer).wait_send()


def collect(source, bank, weights, n, ident):
    rows = up16(-(-HW // n))
    holders = HW // rows
    any_spec = pl.BlockSpec(memory_space=pl.ANY)
    dma = pltpu.SemaphoreType.DMA
    return pl.pallas_call(
        functools.partial(collect_kernel, n, rows, holders),
        out_shape=(
            jax.ShapeDtypeStruct((holders, rows, C), jnp.bfloat16),
            jax.ShapeDtypeStruct((n,) + weights.shape, jnp.bfloat16),
        ),
        in_specs=[pl.BlockSpec(memory_space=pltpu.SMEM), any_spec, any_spec],
        out_specs=(any_spec, any_spec),
        scratch_shapes=[
            pltpu.VMEM((n, rows, C), jnp.bfloat16),
            pltpu.VMEM((rows, C), jnp.bfloat16),
            dma((n,)), dma((n,)),
            dma((3, n)), dma((3, n)),
            dma((n,)), dma((n,)),
            dma((2,)),
        ],
        compiler_params=pltpu.CompilerParams(collective_id=ident, has_side_effects=True),
    )(source, bank, weights)


def heads_of(queries, keys, values, bias):
    lane = lax.broadcasted_iota(jnp.int32, (1, WIDE), 1)
    blocks = [None] * (WIDE // 128)
    for head, (low, high) in enumerate(SPANS):
        inside = (lane >= head * HEAD_DIM) & (lane < (head + 1) * HEAD_DIM)
        inside = inside[:, low * 128 : high * 128]
        q = queries(low, high)
        q = jnp.where(inside, q, jnp.zeros_like(q))
        raw = dot_t(q, keys(low, high))
        if bias is not None:
            raw = raw + bias
        expo = jnp.exp2((raw - jnp.max(raw, axis=-1, keepdims=True)) * FACTOR)
        total = jnp.sum(expo, axis=-1, keepdims=True)
        weights = (expo * (1.0 / total)).astype(jnp.bfloat16)
        part = jnp.where(inside, dot(weights, values(low, high)), 0.0)
        for b in range(low, high):
            piece = part[:, (b - low) * 128 : (b - low + 1) * 128]
            blocks[b] = piece if blocks[b] is None else blocks[b] + piece
    return jnp.concatenate(blocks, axis=1).astype(jnp.bfloat16)


def spatial_kernel(step, lat_ref, w_ref, picked_ref, first_ref, hid_ref, qs, ks, vs):
    @pl.when(pl.program_id(0) == 0)
    def _():
        hidden = normalize(picked_ref[...]).astype(jnp.bfloat16)
        ks[HW:, :] = dot(hidden, w_ref[:, WIDE : 2 * WIDE]).astype(jnp.bfloat16)
        vs[HW:, :] = dot(hidden, w_ref[:, 2 * WIDE : 3 * WIDE]).astype(jnp.bfloat16)

    hidden = normalize(lat_ref[0]).astype(jnp.bfloat16)
    qs[...] = dot(hidden, w_ref[:, :WIDE]).astype(jnp.bfloat16)
    ks[:HW, :] = dot(hidden, w_ref[:, WIDE : 2 * WIDE]).astype(jnp.bfloat16)
    vs[:HW, :] = dot(hidden, w_ref[:, 2 * WIDE : 3 * WIDE]).astype(jnp.bfloat16)

    def rows_of(at, carry):
        rows = pl.ds(pl.multiple_of(at * step, step), step)
        attended = heads_of(
            lambda a, b: qs[rows, a * 128 : b * 128],
            lambda a, b: ks[:, a * 128 : b * 128],
            lambda a, b: vs[:, a * 128 : b * 128],
            None,
        )
        mixed = dot_t(attended, w_ref[:, 3 * WIDE :])
        first = (lat_ref[0, rows, :].astype(jnp.float32) + mixed).astype(jnp.bfloat16)
        first_ref[0, rows, :] = first
        hid_ref[0, rows, :] = normalize(first).astype(jnp.bfloat16)
        return carry

    lax.fori_loop(0, HW // step, rows_of, 0)


def spatial(latents, weights, picked):
    frames = latents.shape[0]
    block = pl.BlockSpec((1, HW, C), lambda f: (f, 0, 0))
    shape = jax.ShapeDtypeStruct(latents.shape, jnp.bfloat16)
    return pl.pallas_call(
        functools.partial(spatial_kernel, 192),
        grid=(frames,),
        out_shape=(shape, shape),
        in_specs=[
            block,
            pl.BlockSpec((C, 4 * WIDE), lambda f: (0, 0)),
            pl.BlockSpec((HW, C), lambda f: (0, 0)),
        ],
        out_specs=(block, block),
        scratch_shapes=[
            pltpu.VMEM((HW, WIDE), jnp.bfloat16),
            pltpu.VMEM((2 * HW, WIDE), jnp.bfloat16),
            pltpu.VMEM((2 * HW, WIDE), jnp.bfloat16),
        ],
        cost_estimate=pl.CostEstimate(
            flops=9_000_000_000, bytes_accessed=9_000_000, transcendentals=5_400_000
        ),
        compiler_params=pltpu.CompilerParams(vmem_limit_bytes=VMEM_LIMIT),
    )(latents, weights, picked)


def temporal_kernel(group, x_ref, w_ref, bias_ref, out_ref, proj):
    proj[...] = dot(x_ref[...], w_ref[:, : 3 * WIDE]).astype(jnp.bfloat16)
    bias = bias_ref[...]
    for at in range(x_ref.shape[0] // group):
        rows = slice(at * group, (at + 1) * group)
        attended = heads_of(
            lambda a, b: proj[rows, a * 128 : b * 128],
            lambda a, b: proj[rows, WIDE + a * 128 : WIDE + b * 128],
            lambda a, b: proj[rows, 2 * WIDE + a * 128 : 2 * WIDE + b * 128],
            bias,
        )
        out_ref[rows, :] = attended[:, :INNER]


def temporal(x, weights, bias):
    rows = x.shape[0]
    return pl.pallas_call(
        functools.partial(temporal_kernel, bias.shape[0]),
        out_shape=jax.ShapeDtypeStruct((rows, INNER), jnp.bfloat16),
        in_specs=[pl.BlockSpec(memory_space=pltpu.VMEM)] * 3,
        out_specs=pl.BlockSpec(memory_space=pltpu.VMEM),
        scratch_shapes=[pltpu.VMEM((rows, 3 * WIDE), jnp.bfloat16)],
        compiler_params=pltpu.CompilerParams(vmem_limit_bytes=VMEM_LIMIT),
    )(x, weights, bias)


def widen(weights):
    parts = weights.reshape(weights.shape[0], 4, INNER)
    parts = jnp.pad(parts, ((0, 0), (0, 0), (0, WIDE - INNER)))
    return parts.reshape(weights.shape[0], 4 * WIDE)


def body(
    latents, offsets, source_device, reference_bank,
    spatial_in, spatial_out, temporal_in, temporal_out,
):
    n = lax.axis_size("frame")
    frames = latents.shape[0]
    total = n * frames
    spots = HW // n
    depth = spatial_in.shape[0]

    packed_t = jnp.concatenate([temporal_in, temporal_out.T], axis=1)
    gathered_t = lax.all_gather(packed_t, "frame", axis=0, tiled=True)
    starts = lax.all_gather(offsets, "frame", axis=0, tiled=True)

    packed_s = jnp.concatenate([spatial_in, spatial_out.T], axis=1)
    packed_s = jnp.pad(packed_s, ((0, up16(depth) - depth), (0, 0)))
    picked, gathered_s = collect(source_device, reference_bank, packed_s, n, 0)
    weights_s = widen(gathered_s[:, :depth].reshape(C, 4 * INNER))
    first, hidden = spatial(latents, weights_s, picked.reshape(HW, C))

    held = up16(frames * spots)
    x = hidden.reshape(frames, n, spots, C).transpose(1, 0, 2, 3).reshape(n, frames * spots, C)
    x = jnp.pad(x, ((0, 0), (0, held - frames * spots), (0, 0)))
    x = exchange(x, 1)[:, : frames * spots]
    x = x.reshape(total, spots, C).transpose(1, 0, 2).reshape(spots * total, C)

    group = max(128, total)
    row = jnp.arange(group, dtype=jnp.int32)
    time, spot = row % total, row // total
    begin = (time // frames) * frames - (WIN // 2 - 1) + jnp.repeat(
        jnp.tile(starts, group // total), frames
    )
    valid = (
        (spot[:, None] == spot[None, :])
        & (time[None, :] >= begin[:, None])
        & (time[None, :] < begin[:, None] + WIN)
    )
    bias = jnp.where(valid, 0.0, -1e30).astype(jnp.float32)
    back = temporal(x, widen(gathered_t), bias)

    back = back.reshape(spots, n, frames, INNER).transpose(1, 2, 0, 3)
    back = back.reshape(n, frames * spots, INNER)
    back = jnp.pad(back, ((0, 0), (0, held - frames * spots), (0, 0)))
    back = exchange(back, 2)[:, : frames * spots]
    back = back.reshape(n, frames, spots, INNER).transpose(1, 0, 2, 3).reshape(frames * HW, INNER)
    second = dot_t(back, gathered_t[:, 3 * INNER :])
    blended = (first.astype(jnp.float32).reshape(frames * HW, C) + second).astype(jnp.bfloat16)
    return blended.reshape(frames, HW, C)


def solution(mesh):
    placed = (
        P(("clip", "frame"), None, None),
        P(("clip", "frame")),
        P("clip"),
        P(("clip", "frame"), None, None),
        P("frame", None),
        P(None, "frame"),
        P("frame", None),
        P(None, "frame"),
    )
    return jax.shard_map(
        body, mesh=mesh, in_specs=placed,
        out_specs=P(("clip", "frame"), None, None), check_vma=False,
    )
```

time: 471 us -> 238 us (0.51)
  waiting for transfers between devices: 226 us -> 0.02 us
  Pallas kernels: 0 us -> 165 us
  local copies, waits for them, and re-layouts: 85.7 us -> 33.1 us
  matrix products: 54.6 us -> 3.22 us
  blocking collectives: 61.1 us -> 13.7 us
  starting transfers between devices: 17.9 us -> 0.01 us
  other arithmetic: 9.55 us -> 4.03 us
    pallas_call x0 -> x5, Pallas kernels: none -> 165 us  [the longest x2 68.7 us: exchange(): pl.pallas_call(functools.partial(exchange_kernel, n), out_shape=jax.Shape...]
    ppermute x8 -> x0, waiting for transfers between devices: 116 us -> none  [shifted(): lax.ppermute(value, axis, [(source, source + steps) for source in range(f...]
    psum x1 -> x0, waiting for transfers between devices: 68 us -> none  [broadcast(): return lax.psum(block, axis)]
    all_gather x2 -> x0, blocking collectives: 61.1 us -> none  [the longest x1 35.5 us: body(): lax.all_gather(temporal_out, 'frame', axis=1, tiled=True)]
    all_gather x2 -> x1, waiting for transfers between devices: 40.6 us -> 0.01 us  [body(): gathered_t = lax.all_gather(packed_t, 'frame', axis=0, tiled=True)]
    reshape x3 -> x7, local copies, waits for them, and re-layouts: 32.9 us -> 6 us  [the longest x1 2.41 us: widen(): return parts.reshape(weights.shape[0], 4 * WIDE)]
    sub x3 -> x0, matrix products: 26.1 us -> none  [softmax_rounded(): scores = scores - jnp.max(scores, axis=-1, keepdims=True)]
    slice x7 -> x6, local copies, waits for them, and re-layouts: 31 us -> 5.38 us  [the longest x1 2.73 us: body(): weights_s = widen(gathered_s[:, :depth].reshape(C, 4 * INNER))]
  transfers between devices with their start and end apart: 11 -> 1, of which waited for: 6 -> 0; matrix products, arithmetic and copies ran while one was open for 12% -> 9% of each run, Pallas kernels for 0% -> 53%
where the time goes in v1:
time: 238 us; the launch traced here: 234 us
  Pallas kernels  165 us (69%)
  local copies, waits for them, and re-layouts  33.1 us (14%)
  between operations  14.9 us (6%)
  blocking collectives  13.7 us (6%)
  other arithmetic  4.03 us (2%)
  matrix products  3.22 us (1%)
    pallas_call x2, Pallas kernels, exchange(): pl.pallas_call(functools.partial(exchange_kernel, n), out_shape=jax.Shape...  68.7 us
    pallas_call x1, Pallas kernels, collect(): pl.pallas_call(functools.partial(collect_kernel, n, rows, holders), out_s...  58.2 us
    pallas_call x1, Pallas kernels, spatial(): pl.pallas_call(functools.partial(spatial_kernel, 192), grid=(frames,), ou...  25.3 us
    unnamed x1, blocking collectives  13.7 us
    pallas_call x1, Pallas kernels, temporal(): pl.pallas_call(functools.partial(temporal_kernel, bias.shape[0]), out_sha...  12.5 us
  transfers between devices with their start and end apart: 1, of which 0 were waited for; matrix products, arithmetic and copies ran while one was open for 9% of the time, Pallas kernels for 53%

profile of v1, /device:TPU:0, one launch (start us, length us, event | category | flops | bytes accessed | tf_op | source)
XLA Modules:
  0.0 233.6 jit_solution(13095078942791939200)
XLA Ops:
  6.5 1.6 pad_maximum_fusion
  8.8 1.2 dynamic-slice
  10.1 0.8 dynamic-update-slice
  10.8 13.7 %all-reduce.5 = s32[16]{0:T(128)S(1)} all-reduce(s32[16]{0:T(128)S(1)} %dynamic-update-slice), channel_id=1, replica_groups=mesh['frame'=16,'clip'=2] {'frame'}, use_global_device_ids=true, to_apply=%add.5 | all-reduce | flops 16 | bytes 128
  25.2 1.6 fusion.4.w_ref
  26.9 58.2 %shard_map.82 = (bf16[12,48,640]{2,1,0:T(8,128)(2,1)}, bf16[16,48,1280]{2,1,0:T(8,128)(2,1)}) custom-call(s32[1]{0:T(128)S(6)} %copy.37.src_ref, bf16[1,576,640]{2,1,0:T(8,128)(2,1)} %bank_ref.1, bf16[48,1280]{1,0:T(8,128)(2,1)} %fusion.4.w_ref), custom_call_target="tpu_custom_call" | custom-call | tf_op jit(solution)/shard_map/pallas_call | solution.py:205
  85.1 2.7 %slice.12 = bf16[16,40,1280]{2,1,0:T(8,128)(2,1)} slice(bf16[16,48,1280]{2,1,0:T(8,128)(2,1)} %get-tuple-element.9), slice={[0:16], [0:40], [0:1280]} | slice | bytes 3276800 | tf_op jit(solution)/shard_map/slice | solution.py:350
  87.8 4.2 %reshape_reshape.3 = bf16[640,4,320]{2,1,0:T(4,128)(2,1)S(1)} reshape(bf16[16,40,1280]{2,1,0:T(8,128)(2,1)} %slice.12) | data formatting | bytes 3276800 | tf_op jit(solution)/shard_map/reshape;reshape | solution.py:328
  92.0 0.8 pad.20
  92.8 1.6 copy.34
  94.4 25.3 %shard_map.83 = (bf16[2,576,640]{2,1,0:T(8,128)(2,1)}, bf16[2,576,640]{2,1,0:T(8,128)(2,1)}) custom-call(bf16[2,576,640]{2,1,0:T(8,128)(2,1)} %lat_ref.1, bf16[640,1536]{1,0:T(8,128)(2,1)} %bitcast.33, bf16[576,640]{1,0:T(8,128)(2,1)} %bitcast.37), custom_call_target="tpu_custom_call" | custom-call | flops 8999999488 | bytes 9000000 | tf_op jit(solution)/shard_map/pallas_call | solution.py:279
  119.7 2.9 %copy.23 = bf16[2,576,640]{2,0,1:T(2,128)(2,1)S(1)} copy(bf16[2,576,640]{2,1,0:T(8,128)(2,1)} %get-tuple-element.12) | data formatting | bytes 2949120 | tf_op jit(solution)/shard_map/pallas_call | solution.py:279
  122.8 0.3 copy.25
  123.1 1.3 pad.21.x_ref
  124.4 39.2 %shard_map.84 = bf16[16,80,640]{2,1,0:T(8,128)(2,1)} custom-call(bf16[16,80,640]{2,1,0:T(8,128)(2,1)} %pad.21.x_ref), custom_call_target="tpu_custom_call" | custom-call | tf_op jit(solution)/shard_map/pallas_call | solution.py:79
  163.6 1.4 slice-done
  165.0 0.3 reshape.128
  165.3 1.3 copy.26
  167.0 0.7 and_select_fusion.bias_ref
  167.7 3.5 %copy.27 = bf16[640,1280]{0,1:T(8,128)(2,1)} copy(bf16[640,1280]{1,0:T(8,128)(2,1)} %all-gather.2.cloned.1.call-done) | data formatting | bytes 3276800 | tf_op jit(solution)/shard_map/all_gather | solution.py:344
  171.2 1.6 pad.22
  172.8 2.4 %copy.33.w_ref = bf16[640,1536]{1,0:T(8,128)(2,1)} copy(bf16[640,1536]{0,1:T(8,128)(2,1)S(1)} %bitcast.24) | data formatting | bytes 3932160 | tf_op jit(solution)/shard_map/reshape | solution.py:330
  175.2 12.5 %shard_map.85 = bf16[1152,320]{1,0:T(8,128)(2,1)} custom-call(bf16[1152,640]{1,0:T(8,128)(2,1)} %bitcast.27, bf16[640,1536]{1,0:T(8,128)(2,1)} %copy.33.w_ref, f32[128,128]{1,0:T(8,128)} %and_select_fusion.bias_ref), custom_call_target="tpu_custom_call" | custom-call | tf_op jit(solution)/shard_map/pallas_call | solution.py:317
  187.8 2.3 reshape.133
  190.2 0.2 copy.30
  190.4 1.0 pad.23.x_ref
  191.4 29.5 %shard_map.86 = bf16[16,80,320]{2,1,0:T(8,128)(2,1)} custom-call(bf16[16,80,320]{2,1,0:T(8,128)(2,1)} %pad.23.x_ref), custom_call_target="tpu_custom_call" | custom-call | tf_op jit(solution)/shard_map/pallas_call | solution.py:79
  220.9 1.2 slice-done.1
  222.2 0.2 copy.32
  222.4 0.4 reshape.136
  222.8 0.8 copy-done
  223.5 3.2 %fusion = bf16[1152,640]{1,0:T(8,128)(2,1)} fusion(bf16[1152,320]{1,0:T(8,128)(2,1)S(1)} %reshape.136, bf16[1152,640]{1,0:T(8,128)(2,1)S(1)} %bitcast.34, bf16[640,1280]{1,0:T(8,128)(2,1)} %all-gather.2.cloned.1.call-done), kind=kOutput, calls=%fused_computation.1 | convolution fusion | flops 474071040 | bytes 4177920 | tf_op jit(solution)/shard_map/dot_general | solution.py:42
  (16 shorter events, 0.8 us)
Async XLA Ops:
  6.5 161.2 %all-gather.2.cloned.1.call-start = ((), (), s32[]{:S(2)}) async-start(), calls=%async_computation | async-start | bytes 1740800 | tf_op jit(solution)/shard_map/all_gather | solution.py:344
  163.6 1.4 slice-start
  220.9 1.2 slice-start.1
  222.2 1.4 copy-start
Sparse Core Ops, SparseCore 0:
  9.5 53.6 all-gather.1

commit v2 on v1

--- a/solution.py
+++ b/solution.py
@@ -15,6 +15,9 @@
 INNER = 320
 WIDE = 384
 WIN = 16
+PLANE = 4
+CLUSTER = 16
+PIECES = 3
 MESH = pl.DeviceIdType.MESH
 FACTOR = HEAD_DIM ** (-0.5) * math.log2(math.e)
 VMEM_LIMIT = 60 * 1024 * 1024
@@ -56,38 +59,6 @@
             barrier, inc=1, device_id={"frame": lax.rem(me + k, n)}, device_id_type=MESH
         )
     pl.semaphore_wait(barrier, n - 1)
-
-
-def exchange_kernel(n, x_ref, o_ref, send, recv, local):
-    me = lax.axis_index("frame")
-    greet(n, me)
-    copies = []
-    for k in range(1, n):
-        peer = lax.rem(me + k, n)
-        copy = remote(x_ref.at[peer], o_ref.at[me], send.at[k], recv.at[k], peer)
-        copy.start()
-        copies.append(copy)
-    own = pltpu.make_async_copy(x_ref.at[me], o_ref.at[me], local)
-    own.start()
-    own.wait()
-    for copy in copies:
-        copy.wait()
-
-
-def exchange(x, ident):
-    n = x.shape[0]
-    return pl.pallas_call(
-        functools.partial(exchange_kernel, n),
-        out_shape=jax.ShapeDtypeStruct(x.shape, x.dtype),
-        in_specs=[pl.BlockSpec(memory_space=pl.ANY)],
-        out_specs=pl.BlockSpec(memory_space=pl.ANY),
-        scratch_shapes=[
-            pltpu.SemaphoreType.DMA((n,)),
-            pltpu.SemaphoreType.DMA((n,)),
-            pltpu.SemaphoreType.DMA,
-        ],
-        compiler_params=pltpu.CompilerParams(collective_id=ident, has_side_effects=True),
-    )(x)
 
 
 def collect_kernel(
@@ -243,85 +214,255 @@
     return jnp.concatenate(blocks, axis=1).astype(jnp.bfloat16)
 
 
-def spatial_kernel(step, lat_ref, w_ref, picked_ref, first_ref, hid_ref, qs, ks, vs):
-    @pl.when(pl.program_id(0) == 0)
+def block_kernel(
+    n, lat_ref, ws_ref, picked_ref, wt_ref, off_ref, out_ref,
+    qs, ks, vs, firsts, outgoing, hall, tproj, bias, tatt, back,
+    psend, precv, zsend, zrecv, bsend, brecv,
+):
+    me = lax.axis_index("frame")
+    levels = n // PLANE
+    level, sub = me // PLANE, lax.rem(me, PLANE)
+    base = level * PLANE
+    frames = lat_ref.shape[0]
+    spots = HW // PLANE
+    barrier = pltpu.get_barrier_semaphore()
+    has_down, has_up = level > 0, level < levels - 1
+
+    def signal(peer):
+        pl.semaphore_signal(barrier, inc=1, device_id={"frame": peer}, device_id_type=MESH)
+
+    def mate(k):
+        return base + lax.rem(sub + 1 + k, PLANE)
+
+    for k in range(PLANE - 1):
+        signal(mate(k))
+
+    @pl.when(has_up)
     def _():
-        hidden = normalize(picked_ref[...]).astype(jnp.bfloat16)
-        ks[HW:, :] = dot(hidden, w_ref[:, WIDE : 2 * WIDE]).astype(jnp.bfloat16)
-        vs[HW:, :] = dot(hidden, w_ref[:, 2 * WIDE : 3 * WIDE]).astype(jnp.bfloat16)
-
-    hidden = normalize(lat_ref[0]).astype(jnp.bfloat16)
-    qs[...] = dot(hidden, w_ref[:, :WIDE]).astype(jnp.bfloat16)
-    ks[:HW, :] = dot(hidden, w_ref[:, WIDE : 2 * WIDE]).astype(jnp.bfloat16)
-    vs[:HW, :] = dot(hidden, w_ref[:, 2 * WIDE : 3 * WIDE]).astype(jnp.bfloat16)
-
-    def rows_of(at, carry):
-        rows = pl.ds(pl.multiple_of(at * step, step), step)
+        signal(me + PLANE)
+
+    @pl.when(has_down)
+    def _():
+        signal(me - PLANE)
+
+    pl.semaphore_wait(
+        barrier, PLANE - 1 + has_up.astype(jnp.int32) + has_down.astype(jnp.int32)
+    )
+
+    @pl.when(level == 0)
+    def _():
+        hall[0] = jnp.zeros(hall.shape[1:], jnp.bfloat16)
+
+    @pl.when(level == levels - 1)
+    def _():
+        hall[2] = jnp.zeros(hall.shape[1:], jnp.bfloat16)
+
+    def send_plane(f, k):
+        return remote(
+            outgoing.at[f, k], hall.at[1, frames * sub + f],
+            psend.at[f, k], precv.at[f, k], base + lax.rem(sub + 1 + k, PLANE),
+        )
+
+    def arrived(f, k):
+        source = lax.rem(sub + 2 * PLANE - 1 - k, PLANE)
+        return frames * source + f
+
+    def send_level(f, k, up):
+        at = arrived(f, k)
+        side = 0 if up else 1
+        return remote(
+            hall.at[1, at], hall.at[0 if up else 2, at],
+            zsend.at[side, f, k], zrecv.at[side, f, k], me + PLANE if up else me - PLANE,
+        )
+
+    def pass_on(f, k):
+        @pl.when(has_up)
+        def _():
+            send_level(f, k, True).start()
+
+        @pl.when(has_down)
+        def _():
+            send_level(f, k, False).start()
+
+    hidden = normalize(picked_ref[...]).astype(jnp.bfloat16)
+    ks[HW:, :] = dot(hidden, ws_ref[:, WIDE : 2 * WIDE]).astype(jnp.bfloat16)
+    vs[HW:, :] = dot(hidden, ws_ref[:, 2 * WIDE : 3 * WIDE]).astype(jnp.bfloat16)
+    last = PLANE - 1
+
+    def step(t, carry):
+        f, k = t // PLANE, lax.rem(t, PLANE)
+
+        @pl.when(k == 0)
+        def _():
+            hidden = normalize(lat_ref[f]).astype(jnp.bfloat16)
+            qs[...] = dot(hidden, ws_ref[:, :WIDE]).astype(jnp.bfloat16)
+            ks[:HW, :] = dot(hidden, ws_ref[:, WIDE : 2 * WIDE]).astype(jnp.bfloat16)
+            vs[:HW, :] = dot(hidden, ws_ref[:, 2 * WIDE : 3 * WIDE]).astype(jnp.bfloat16)
+
+        to = lax.rem(sub + 1 + k, PLANE)
+        rows = pl.ds(pl.multiple_of(to * spots, 16), spots)
         attended = heads_of(
             lambda a, b: qs[rows, a * 128 : b * 128],
             lambda a, b: ks[:, a * 128 : b * 128],
             lambda a, b: vs[:, a * 128 : b * 128],
             None,
         )
-        mixed = dot_t(attended, w_ref[:, 3 * WIDE :])
-        first = (lat_ref[0, rows, :].astype(jnp.float32) + mixed).astype(jnp.bfloat16)
-        first_ref[0, rows, :] = first
-        hid_ref[0, rows, :] = normalize(first).astype(jnp.bfloat16)
+        mixed = dot_t(attended, ws_ref[:, 3 * WIDE :])
+        first = (lat_ref[f, rows, :].astype(jnp.float32) + mixed).astype(jnp.bfloat16)
+        firsts[f, rows, :] = first
+        result = normalize(first).astype(jnp.bfloat16)
+
+        @pl.when(k < last)
+        def _():
+            outgoing[f, k] = result
+            send_plane(f, k).start()
+
+        @pl.when(k == last)
+        def _():
+            hall[1, frames * sub + f] = result
+            pass_on(f, last)
+
+        @pl.when(k > 0)
+        def _():
+            send_plane(f, k - 1).wait_recv()
+            pass_on(f, k - 1)
+
         return carry
 
-    lax.fori_loop(0, HW // step, rows_of, 0)
-
-
-def spatial(latents, weights, picked):
+    lax.fori_loop(0, frames * PLANE, step, 0)
+
+    time = PLANE * frames
+    row = lax.broadcasted_iota(jnp.int32, bias.shape, 0)
+    col = lax.broadcasted_iota(jnp.int32, bias.shape, 1)
+    mine = row // CLUSTER
+    begin = mine // frames * frames - (WIN // 2 - 1)
+    for i in range(PLANE):
+        begin = begin + jnp.where(mine // frames == i, off_ref[i], 0)
+    side = col // (CLUSTER * time) - 1
+    other = col // CLUSTER - time
+    valid = (
+        (lax.rem(row, CLUSTER) == lax.rem(col, CLUSTER))
+        & (other >= begin) & (other < begin + WIN)
+        & (level + side >= 0) & (level + side < levels)
+    )
+    bias[...] = jnp.where(valid, 0.0, -1e30)
+
+    def project(at):
+        flat = hall[at].reshape(time * spots, C)
+        low = 0 if at == 1 else WIDE
+        result = dot(flat, wt_ref[:, low : 3 * WIDE]).astype(jnp.bfloat16)
+        tproj[at, :, :, low:] = result.reshape(time, spots, 3 * WIDE - low)
+
+    project(1)
+
+    for f in range(frames):
+        for k in range(PLANE):
+            @pl.when(has_down)
+            def _():
+                send_level(f, k, True).wait_recv()
+
+            @pl.when(has_up)
+            def _():
+                send_level(f, k, False).wait_recv()
+
+    project(0)
+    project(2)
+
+    piece = spots // PIECES
+
+    def send_back(c, k):
+        to = lax.rem(sub + 1 + k, PLANE)
+        rows = pl.ds(pl.multiple_of(c * piece, 16), piece)
+        return remote(
+            tatt.at[pl.ds(frames * to, frames), rows], back.at[sub, :, rows],
+            bsend.at[c, k], brecv.at[c, k], base + to,
+        )
+
+    def temporal(c, carry):
+        for inner in range(piece // CLUSTER):
+            at = pl.multiple_of(c * piece + inner * CLUSTER, CLUSTER)
+            spot = pl.ds(at, CLUSTER)
+
+            def near(low):
+                def get(a, b):
+                    got = tproj[:, :, spot, low + a * 128 : low + b * 128]
+                    return got.reshape(3 * time * CLUSTER, (b - a) * 128)
+                return get
+
+            attended = heads_of(
+                lambda a, b: tproj[1, :, spot, a * 128 : b * 128].reshape(
+                    time * CLUSTER, (b - a) * 128
+                ),
+                near(WIDE), near(2 * WIDE), bias[...],
+            )
+            tatt[:, spot, :] = attended.reshape(time, CLUSTER, WIDE)
+        for k in range(last):
+            send_back(c, k).start()
+        return carry
+
+    lax.fori_loop(0, PIECES, temporal, 0)
+
+    def finish(which, values):
+        rows = pl.ds(pl.multiple_of(which * spots, 16), spots)
+        for f in range(frames):
+            second = dot_t(values(f), wt_ref[:, 3 * WIDE :])
+            out_ref[f, rows, :] = (firsts[f, rows, :].astype(jnp.float32) + second).astype(
+                jnp.bfloat16
+            )
+
+    finish(sub, lambda f: tatt[frames * sub + f])
+    for k in range(last):
+        for c in range(PIECES):
+            send_back(c, k).wait_recv()
+        source = lax.rem(sub + PLANE - 1 - k, PLANE)
+        finish(source, lambda f: back[source, f])
+    for k in range(last):
+        for c in range(PIECES):
+            send_back(c, k).wait_send()
+        for f in range(frames):
+            send_plane(f, k).wait_send()
+    for f in range(frames):
+        for k in range(PLANE):
+            @pl.when(has_up)
+            def _():
+                send_level(f, k, True).wait_send()
+
+            @pl.when(has_down)
+            def _():
+                send_level(f, k, False).wait_send()
+
+
+def block(latents, ws, picked, wt, offs, n, ident):
     frames = latents.shape[0]
-    block = pl.BlockSpec((1, HW, C), lambda f: (f, 0, 0))
-    shape = jax.ShapeDtypeStruct(latents.shape, jnp.bfloat16)
+    spots = HW // PLANE
+    time = PLANE * frames
+    vmem = pl.BlockSpec(memory_space=pltpu.VMEM)
+    dma = pltpu.SemaphoreType.DMA
+    bf = jnp.bfloat16
     return pl.pallas_call(
-        functools.partial(spatial_kernel, 192),
-        grid=(frames,),
-        out_shape=(shape, shape),
-        in_specs=[
-            block,
-            pl.BlockSpec((C, 4 * WIDE), lambda f: (0, 0)),
-            pl.BlockSpec((HW, C), lambda f: (0, 0)),
+        functools.partial(block_kernel, n),
+        out_shape=jax.ShapeDtypeStruct(latents.shape, bf),
+        in_specs=[vmem] * 4 + [pl.BlockSpec(memory_space=pltpu.SMEM)],
+        out_specs=vmem,
+        scratch_shapes=[
+            pltpu.VMEM((HW, WIDE), bf),
+            pltpu.VMEM((2 * HW, WIDE), bf),
+            pltpu.VMEM((2 * HW, WIDE), bf),
+            pltpu.VMEM((frames, HW, C), bf),
+            pltpu.VMEM((frames, PLANE - 1, spots, C), bf),
+            pltpu.VMEM((3, time, spots, C), bf),
+            pltpu.VMEM((3, time, spots, 3 * WIDE), bf),
+            pltpu.VMEM((time * CLUSTER, 3 * time * CLUSTER), jnp.float32),
+            pltpu.VMEM((time, spots, WIDE), bf),
+            pltpu.VMEM((PLANE, frames, spots, WIDE), bf),
+            dma((frames, PLANE)), dma((frames, PLANE)),
+            dma((2, frames, PLANE)), dma((2, frames, PLANE)),
+            dma((PIECES, PLANE)), dma((PIECES, PLANE)),
         ],
-        out_specs=(block, block),
-        scratch_shapes=[
-            pltpu.VMEM((HW, WIDE), jnp.bfloat16),
-            pltpu.VMEM((2 * HW, WIDE), jnp.bfloat16),
-            pltpu.VMEM((2 * HW, WIDE), jnp.bfloat16),
-        ],
-        cost_estimate=pl.CostEstimate(
-            flops=9_000_000_000, bytes_accessed=9_000_000, transcendentals=5_400_000
+        compiler_params=pltpu.CompilerParams(
+            collective_id=ident, has_side_effects=True, vmem_limit_bytes=VMEM_LIMIT
         ),
-        compiler_params=pltpu.CompilerParams(vmem_limit_bytes=VMEM_LIMIT),
-    )(latents, weights, picked)
-
-
-def temporal_kernel(group, x_ref, w_ref, bias_ref, out_ref, proj):
-    proj[...] = dot(x_ref[...], w_ref[:, : 3 * WIDE]).astype(jnp.bfloat16)
-    bias = bias_ref[...]
-    for at in range(x_ref.shape[0] // group):
-        rows = slice(at * group, (at + 1) * group)
-        attended = heads_of(
-            lambda a, b: proj[rows, a * 128 : b * 128],
-            lambda a, b: proj[rows, WIDE + a * 128 : WIDE + b * 128],
-            lambda a, b: proj[rows, 2 * WIDE + a * 128 : 2 * WIDE + b * 128],
-            bias,
-        )
-        out_ref[rows, :] = attended[:, :INNER]
-
-
-def temporal(x, weights, bias):
-    rows = x.shape[0]
-    return pl.pallas_call(
-        functools.partial(temporal_kernel, bias.shape[0]),
-        out_shape=jax.ShapeDtypeStruct((rows, INNER), jnp.bfloat16),
-        in_specs=[pl.BlockSpec(memory_space=pltpu.VMEM)] * 3,
-        out_specs=pl.BlockSpec(memory_space=pltpu.VMEM),
-        scratch_shapes=[pltpu.VMEM((rows, 3 * WIDE), jnp.bfloat16)],
-        compiler_params=pltpu.CompilerParams(vmem_limit_bytes=VMEM_LIMIT),
-    )(x, weights, bias)
+    )(latents, ws, picked, wt, offs)
 
 
 def widen(weights):
@@ -335,49 +476,22 @@
     spatial_in, spatial_out, temporal_in, temporal_out,
 ):
     n = lax.axis_size("frame")
-    frames = latents.shape[0]
-    total = n * frames
-    spots = HW // n
     depth = spatial_in.shape[0]
-
-    packed_t = jnp.concatenate([temporal_in, temporal_out.T], axis=1)
-    gathered_t = lax.all_gather(packed_t, "frame", axis=0, tiled=True)
-    starts = lax.all_gather(offsets, "frame", axis=0, tiled=True)
-
-    packed_s = jnp.concatenate([spatial_in, spatial_out.T], axis=1)
-    packed_s = jnp.pad(packed_s, ((0, up16(depth) - depth), (0, 0)))
-    picked, gathered_s = collect(source_device, reference_bank, packed_s, n, 0)
-    weights_s = widen(gathered_s[:, :depth].reshape(C, 4 * INNER))
-    first, hidden = spatial(latents, weights_s, picked.reshape(HW, C))
-
-    held = up16(frames * spots)
-    x = hidden.reshape(frames, n, spots, C).transpose(1, 0, 2, 3).reshape(n, frames * spots, C)
-    x = jnp.pad(x, ((0, 0), (0, held - frames * spots), (0, 0)))
-    x = exchange(x, 1)[:, : frames * spots]
-    x = x.reshape(total, spots, C).transpose(1, 0, 2).reshape(spots * total, C)
-
-    group = max(128, total)
-    row = jnp.arange(group, dtype=jnp.int32)
-    time, spot = row % total, row // total
-    begin = (time // frames) * frames - (WIN // 2 - 1) + jnp.repeat(
-        jnp.tile(starts, group // total), frames
+    held = up16(depth + 1)
+
+    packed_t = widen(jnp.concatenate([temporal_in, temporal_out.T], axis=1))
+    wt = lax.all_gather(packed_t, "frame", axis=0, tiled=True)
+
+    packed_s = widen(jnp.concatenate([spatial_in, spatial_out.T], axis=1))
+    mark = jnp.broadcast_to(offsets.astype(jnp.bfloat16)[:, None], (1, 4 * WIDE))
+    packed_s = jnp.concatenate(
+        [packed_s, mark, jnp.zeros((held - depth - 1, 4 * WIDE), jnp.bfloat16)], axis=0
     )
-    valid = (
-        (spot[:, None] == spot[None, :])
-        & (time[None, :] >= begin[:, None])
-        & (time[None, :] < begin[:, None] + WIN)
-    )
-    bias = jnp.where(valid, 0.0, -1e30).astype(jnp.float32)
-    back = temporal(x, widen(gathered_t), bias)
-
-    back = back.reshape(spots, n, frames, INNER).transpose(1, 2, 0, 3)
-    back = back.reshape(n, frames * spots, INNER)
-    back = jnp.pad(back, ((0, 0), (0, held - frames * spots), (0, 0)))
-    back = exchange(back, 2)[:, : frames * spots]
-    back = back.reshape(n, frames, spots, INNER).transpose(1, 0, 2, 3).reshape(frames * HW, INNER)
-    second = dot_t(back, gathered_t[:, 3 * INNER :])
-    blended = (first.astype(jnp.float32).reshape(frames * HW, C) + second).astype(jnp.bfloat16)
-    return blended.reshape(frames, HW, C)
+    picked, gathered = collect(source_device, reference_bank, packed_s, n, 0)
+    ws = gathered[:, :depth].reshape(C, 4 * WIDE)
+    level = lax.axis_index("frame") // PLANE
+    offs = lax.dynamic_slice_in_dim(gathered[:, depth, 0], level * PLANE, PLANE, 0)
+    return block(latents, ws, picked.reshape(HW, C), wt, offs.astype(jnp.int32), n, 1)
 
 
 def solution(mesh):

time: 238 us -> 167 us (0.70); the launches traced: 234 us -> 167 us
  local copies, waits for them, and re-layouts: 33.1 us -> 7.61 us
  Pallas kernels: 165 us -> 141 us
  blocking collectives: 13.7 us -> 0 us
  matrix products: 3.22 us -> 0 us
    pallas_call x4 -> x1, Pallas kernels: 106 us -> 75.1 us  [block(): pl.pallas_call(functools.partial(block_kernel, n), out_shape=jax.ShapeDty...]
    unnamed x1 -> x0, blocking collectives: 13.7 us -> none
    pallas_call x1, Pallas kernels: 58.2 us -> 66.1 us  [collect(): pl.pallas_call(functools.partial(collect_kernel, n, rows, holders), out_s...]
    reshape x7 -> x2, local copies, waits for them, and re-layouts: 6 us -> 0.34 us  [widen(): parts = weights.reshape(weights.shape[0], 4, INNER)]
    another operation x3 -> x0, local copies, waits for them, and re-layouts: 4.25 us -> none  [the longest x1 4.17 us: widen(): parts = weights.reshape(weights.shape[0], 4, INNER)]
    all_gather x1 -> x0, local copies, waits for them, and re-layouts: 3.54 us -> none  [body(): gathered_t = lax.all_gather(packed_t, 'frame', axis=0, tiled=True)]
    dot_general x1 -> x0, matrix products: 3.22 us -> none  [dot_t(): lax.dot_general(a, b, (((1,), (1,)), ((), ())), preferred_element_type=jn...]
    pallas_call x1 -> x0, local copies, waits for them, and re-layouts: 2.89 us -> none  [spatial(): pl.pallas_call(functools.partial(spatial_kernel, 192), grid=(frames,), ou...]
  transfers between devices with their start and end apart: 1 -> 1, of which waited for: 0 -> 0; matrix products, arithmetic and copies ran while one was open for 9% -> 4% of each run, Pallas kernels for 53% -> 40%
where the time goes in v2:
time: 167 us
  Pallas kernels  141 us (84%)
  between operations  14.8 us (9%)
  local copies, waits for them, and re-layouts  7.61 us (5%)
  other arithmetic  3.41 us (2%)
    pallas_call x1, Pallas kernels, block(): pl.pallas_call(functools.partial(block_kernel, n), out_shape=jax.ShapeDty...  75.1 us
    pallas_call x1, Pallas kernels, collect(): pl.pallas_call(functools.partial(collect_kernel, n, rows, holders), out_s...  66.1 us
  transfers between devices with their start and end apart: 1, of which 0 were waited for; matrix products, arithmetic and copies ran while one was open for 4% of the time, Pallas kernels for 40%

profile of v2, /device:TPU:0, one launch (start us, length us, event | category | flops | bytes accessed | tf_op | source)
XLA Modules:
  0.0 167.0 jit_solution(16179535010891103802)
XLA Ops:
  6.5 0.0 all-gather.2.cloned.1.call-start
  6.5 1.0 pad_maximum_fusion.1
  7.5 0.2 reshape.28
  7.7 0.1 pad.8
  7.8 0.7 copy.10
  8.4 0.0 all-gather.2.cloned.1.call-update
  8.5 1.0 pad_maximum_fusion
  9.4 0.2 reshape.24
  9.6 0.1 pad.7
  10.4 0.1 pad.12.clone
  10.4 0.1 pad.13.clone
  11.2 0.8 maximum_maximum_fusion.w_ref
  11.9 66.1 %shard_map.82 = (bf16[12,48,640]{2,1,0:T(8,128)(2,1)}, bf16[16,48,1536]{2,1,0:T(8,128)(2,1)}) custom-call(s32[1]{0:T(128)S(6)} %copy.13.src_ref, bf16[1,576,640]{2,1,0:T(8,128)(2,1)} %bank_ref.1, bf16[48,1536]{1,0:T(8,128)(2,1)} %maximum_maximum_fusion.w_ref), custom_call_target="tpu_custom_call" | custom-call | tf_op jit(solution)/shard_map/pallas_call | solution.py:176
  78.1 0.8 slice.7
  78.8 3.0 %slice.6 = bf16[16,40,1536]{2,1,0:T(8,128)(2,1)} slice(bf16[16,48,1536]{2,1,0:T(8,128)(2,1)} %get-tuple-element.7), slice={[0:16], [0:40], [0:1536]} | slice | bytes 3932160 | tf_op jit(solution)/shard_map/slice | solution.py:491
  81.8 0.7 convert_reduce_fusion.off_ref
  82.5 0.0 all-gather.2.cloned.1.call-done.wt_ref
  82.5 75.1 %shard_map.83 = bf16[2,576,640]{2,1,0:T(8,128)(2,1)} custom-call(bf16[2,576,640]{2,1,0:T(8,128)(2,1)} %lat_ref.1, bf16[640,1536]{1,0:T(8,128)(2,1)} %bitcast.9, bf16[576,640]{1,0:T(8,128)(2,1)} %bitcast.10, bf16[640,1536]{1,0:T(8,128)(2,1)} %all-gather.2.cloned.1.call-done.wt_ref, s32[4]{0:T(128)} %convert_reduce_fusion.off_ref), custom_call_target="tpu_custom_call" | custom-call | tf_op jit(solution)/shard_map/pallas_call | solution.py:442
  157.6 2.6 %copy.14 = bf16[2,576,640]{2,1,0:T(8,128)(2,1)} copy(bf16[2,576,640]{2,1,0:T(8,128)(2,1)} %shard_map.83) | data formatting | bytes 2949120
  (2 shorter events, 0.0 us)
Async XLA Ops:
  6.5 76.0 %all-gather.2.cloned.1.call-start = ((), (), s32[]{:S(2)}) async-start(), calls=%async_computation | async-start | bytes 2088960 | tf_op jit(solution)/shard_map/all_gather | solution.py:483
Sparse Core Ops, SparseCore 0:
  9.6 60.8 all-gather.1

commit v3 on v2

--- a/solution.py
+++ b/solution.py
@@ -52,142 +52,211 @@
     )
 
 
-def greet(n, me):
-    barrier = pltpu.get_barrier_semaphore()
-    for k in range(1, n):
-        pl.semaphore_signal(
-            barrier, inc=1, device_id={"frame": lax.rem(me + k, n)}, device_id_type=MESH
-        )
-    pl.semaphore_wait(barrier, n - 1)
+def same_chip(me):
+    return me + 1 - 2 * lax.rem(me, 2)
+
+
+def across(me):
+    return me // PLANE * PLANE + lax.rem(lax.rem(me, PLANE) + 2, PLANE)
+
+
+class Relay:
+    def __init__(self, n, wall, send, recv):
+        self.n, self.levels = n, n // PLANE
+        self.wall, self.send, self.recv = wall, send, recv
+        self.me = lax.axis_index("frame")
+        self.mates = (None, across(self.me), same_chip(self.me))
+
+    def along(self, k):
+        part = self.wall.at[self.me]
+        return remote(
+            part, part, self.send.at[0, k], self.recv.at[0, k],
+            lax.rem(self.me + PLANE * k, self.n),
+        )
+
+    def hop(self, stage, origin, k, slot):
+        part = self.wall.at[lax.rem(origin + self.n - PLANE * k, self.n)]
+        return remote(
+            part, part, self.send.at[stage, slot], self.recv.at[stage, slot], self.mates[stage]
+        )
+
+    def begin(self):
+        for k in range(1, self.levels):
+            self.along(k).start()
+        self.hop(1, self.me, 0, 0).start()
+        self.hop(2, self.me, 0, 0).start()
+
+    def second(self):
+        for k in range(1, self.levels):
+            self.along(k).wait_recv()
+            self.hop(1, self.me, k, k).start()
+            self.hop(2, self.me, k, k).start()
+
+    def third(self):
+        for k in range(self.levels):
+            self.hop(1, self.mates[1], k, k).wait_recv()
+            self.hop(2, self.mates[1], k, self.levels + k).start()
+
+    def arrive(self):
+        for k in range(self.levels):
+            self.hop(2, self.mates[2], k, k).wait_recv()
+            self.hop(2, across(self.mates[2]), k, self.levels + k).wait_recv()
+
+    def drain(self):
+        for k in range(self.levels):
+            if k:
+                self.along(k).wait_send()
+            self.hop(1, self.me, k, k).wait_send()
+            self.hop(2, self.me, k, k).wait_send()
+            self.hop(2, self.mates[1], k, self.levels + k).wait_send()
 
 
 def collect_kernel(
     n, rows, holders, src_ref, bank_ref, w_ref, ref_ref, wall_ref,
-    got, chunk, bsend, brecv, wsend, wrecv, rsend, rrecv, local,
+    pair, cross, out_x, out_z, got, chunk, csend, crecv, zsend, zrecv, wsend, wrecv, local,
 ):
     me = lax.axis_index("frame")
-    sub, level = lax.rem(me, 4), me // 4
-    levels = n // 4
-    xmate = level * 4 + lax.rem(sub + 2, 4)
-    cmate = me + 1 - 2 * lax.rem(me, 2)
-    greet(n, me)
-    for k in range(1, n):
-        peer = lax.rem(me + k, n)
-
-        @pl.when(peer < holders)
-        def _():
-            start = pl.multiple_of(peer * rows, 16)
+    sub, level = lax.rem(me, PLANE), me // PLANE
+    levels = n // PLANE
+    xmate, cmate = across(me), same_chip(me)
+    spots = HW // PLANE
+    core, side = lax.rem(me, 2), lax.rem(me, PLANE) // 2
+    barrier = pltpu.get_barrier_semaphore()
+    peers = [xmate, cmate] + [lax.rem(me + PLANE * k, n) for k in range(1, levels)]
+    for peer in peers:
+        pl.semaphore_signal(barrier, inc=1, device_id={"frame": peer}, device_id_type=MESH)
+    place = pltpu.make_async_copy(w_ref, wall_ref.at[me], local.at[0])
+    place.start()
+
+    def bank_rows(x, c):
+        start = pl.multiple_of((2 * x + c) * spots, 16)
+        return bank_ref.at[0, pl.ds(start, spots)]
+
+    for x in range(2):
+        pltpu.make_async_copy(bank_rows(x, core), pair.at[1, x], local.at[1 + x]).start()
+    pl.semaphore_wait(barrier, len(peers))
+
+    def core_copy(x):
+        return remote(bank_rows(x, 1 - core), pair.at[0, x], csend.at[x], crecv.at[x], cmate)
+
+    for x in range(2):
+        core_copy(x).start()
+    relay = Relay(n, wall_ref, wsend, wrecv)
+    place.wait()
+    relay.begin()
+    source = src_ref[0]
+    for x in range(2):
+        pltpu.make_async_copy(bank_rows(x, core), pair.at[1, x], local.at[1 + x]).wait()
+        core_copy(x).wait_recv()
+    pick = (source == me).astype(jnp.int32)
+    out_x[...] = pair[pick, 1 - side]
+    x_copy = remote(out_x, cross.at[0], csend.at[2], crecv.at[2], xmate)
+    x_copy.start()
+    cross[1] = pair[pick, side]
+    x_copy.wait_recv()
+    pick = (source // 2 == me // 2).astype(jnp.int32)
+    out_z[...] = cross[pick]
+
+    def spread(k):
+        peer_level = lax.rem(level + k, levels)
+        start = pl.multiple_of(peer_level * rows, 16)
+        return peer_level, remote(
+            out_z.at[pl.ds(start, rows)], got.at[level], zsend.at[0, k], zrecv.at[0, k],
+            lax.rem(me + PLANE * k, n),
+        )
+
+    for k in range(1, levels):
+        @pl.when(lax.rem(level + k, levels) < holders)
+        def _():
+            spread(k)[1].start()
+
+    def gather(k, origin):
+        part = ref_ref.at[sub, origin]
+        return remote(
+            chunk, part, zsend.at[1, k], zrecv.at[1, k], lax.rem(me + PLANE * k, n)
+        )
+
+    @pl.when(level < holders)
+    def _():
+        got[level] = out_z[pl.ds(pl.multiple_of(level * rows, 16), rows), :]
+        for k in range(1, levels):
             remote(
-                bank_ref.at[0, pl.ds(start, rows)], got.at[me], bsend.at[k], brecv.at[k], peer
-            ).start()
-
-    @pl.when(me < holders)
-    def _():
-        start = pl.multiple_of(me * rows, 16)
-        own = pltpu.make_async_copy(bank_ref.at[0, pl.ds(start, rows)], got.at[me], local.at[0])
+                out_z.at[pl.ds(0, rows)], got.at[lax.rem(level + levels - k, levels)],
+                zsend.at[0, k], zrecv.at[0, k], lax.rem(me + PLANE * k, n),
+            ).wait_recv()
+        chunk[...] = got[source // PLANE]
+        for k in range(1, levels):
+            gather(k, level).start()
+        own = pltpu.make_async_copy(chunk, ref_ref.at[sub, level], local.at[1])
         own.start()
         own.wait()
 
-    place = pltpu.make_async_copy(w_ref, wall_ref.at[me], local.at[1])
-    place.start()
-
-    def z_copy(k):
-        peer = lax.rem(me + 4 * k, n)
-        return remote(w_ref, wall_ref.at[me], wsend.at[0, k], wrecv.at[0, k], peer)
-
-    def hop_copy(stage, block, slot, peer):
-        part = wall_ref.at[block]
-        return remote(part, part, wsend.at[stage, slot], wrecv.at[stage, slot], peer)
-
+    relay.second()
     for k in range(1, levels):
-        z_copy(k).start()
-    place.wait()
-    firsts = []
-    for k in range(levels):
-        block = lax.rem(me + n - 4 * k, n)
-        if k:
-            z_copy(k).wait_recv()
-        copy = hop_copy(1, block, k, xmate)
-        copy.start()
-        firsts.append(copy)
-        last = hop_copy(2, block, k, cmate)
-        last.start()
-        firsts.append(last)
-    for k in range(1, n):
-        peer = lax.rem(me + k, n)
-
-        @pl.when(me < holders)
-        def _():
-            start = pl.multiple_of(me * rows, 16)
-            remote(
-                bank_ref.at[0, pl.ds(start, rows)], got.at[me], bsend.at[k], brecv.at[k], peer
-            ).wait_recv()
-
-        @pl.when(peer < holders)
-        def _():
-            start = pl.multiple_of(peer * rows, 16)
-            remote(
-                bank_ref.at[0, pl.ds(start, rows)], got.at[me], bsend.at[k], brecv.at[k], peer
-            ).wait_send()
-
-    @pl.when(me < holders)
-    def _():
-        chunk[...] = got[src_ref[0]]
-        for k in range(1, n):
-            peer = lax.rem(me + k, n)
-            remote(chunk, ref_ref.at[me], rsend.at[k], rrecv.at[k], peer).start()
-        own = pltpu.make_async_copy(chunk, ref_ref.at[me], local.at[0])
-        own.start()
-        own.wait()
-
-    for k in range(levels):
-        block = lax.rem(xmate + n - 4 * k, n)
-        hop_copy(1, block, k, xmate).wait_recv()
-        last = hop_copy(2, block, levels + k, cmate)
-        last.start()
-        firsts.append(last)
-    for k in range(levels):
-        for side in range(2):
-            origin = cmate if side == 0 else lax.rem(cmate // 4 * 4 + lax.rem(cmate + 2, 4), n)
-            block = lax.rem(origin + n - 4 * k, n)
-            hop_copy(2, block, side * levels + k, cmate).wait_recv()
-    for copy in firsts:
-        copy.wait_send()
+        sender = lax.rem(level + levels - k, levels)
+
+        @pl.when(sender < holders)
+        def _():
+            gather(k, sender).wait_recv()
+
+    other = lax.rem(sub + 2, PLANE)
+
+    def plane_copy(which, slot, peer):
+        return remote(
+            ref_ref.at[which], ref_ref.at[which], csend.at[slot], crecv.at[slot], peer
+        )
+
+    plane_copy(sub, 3, xmate).start()
+    plane_copy(sub, 4, cmate).start()
+    relay.third()
+    plane_copy(other, 3, xmate).wait_recv()
+    plane_copy(other, 5, cmate).start()
+    relay.arrive()
+    plane_copy(lax.rem(cmate, PLANE), 4, cmate).wait_recv()
+    plane_copy(lax.rem(across(cmate), PLANE), 5, cmate).wait_recv()
+    relay.drain()
+    for x in range(2):
+        core_copy(x).wait_send()
+    x_copy.wait_send()
+    plane_copy(sub, 3, xmate).wait_send()
+    plane_copy(sub, 4, cmate).wait_send()
+    plane_copy(other, 5, cmate).wait_send()
     for k in range(1, levels):
-        z_copy(k).wait_send()
-    for k in range(1, n):
-        peer = lax.rem(me + k, n)
-        sender = lax.rem(me + n - k, n)
-
-        @pl.when(sender < holders)
-        def _():
-            remote(chunk, ref_ref.at[sender], rsend.at[k], rrecv.at[k], peer).wait_recv()
-
-        @pl.when(me < holders)
-        def _():
-            remote(chunk, ref_ref.at[me], rsend.at[k], rrecv.at[k], peer).wait_send()
+        @pl.when(lax.rem(level + k, levels) < holders)
+        def _():
+            spread(k)[1].wait_send()
+
+        @pl.when(level < holders)
+        def _():
+            gather(k, level).wait_send()
 
 
 def collect(source, bank, weights, n, ident):
-    rows = up16(-(-HW // n))
-    holders = HW // rows
+    spots, levels = HW // PLANE, n // PLANE
+    rows = up16(-(-spots // levels))
+    holders = spots // rows
     any_spec = pl.BlockSpec(memory_space=pl.ANY)
     dma = pltpu.SemaphoreType.DMA
+    bf = jnp.bfloat16
     return pl.pallas_call(
         functools.partial(collect_kernel, n, rows, holders),
         out_shape=(
-            jax.ShapeDtypeStruct((holders, rows, C), jnp.bfloat16),
-            jax.ShapeDtypeStruct((n,) + weights.shape, jnp.bfloat16),
+            jax.ShapeDtypeStruct((PLANE, holders, rows, C), bf),
+            jax.ShapeDtypeStruct((n,) + weights.shape, bf),
         ),
         in_specs=[pl.BlockSpec(memory_space=pltpu.SMEM), any_spec, any_spec],
         out_specs=(any_spec, any_spec),
         scratch_shapes=[
-            pltpu.VMEM((n, rows, C), jnp.bfloat16),
-            pltpu.VMEM((rows, C), jnp.bfloat16),
-            dma((n,)), dma((n,)),
+            pltpu.VMEM((2, 2, spots, C), bf),
+            pltpu.VMEM((2, spots, C), bf),
+            pltpu.VMEM((spots, C), bf),
+            pltpu.VMEM((spots, C), bf),
+            pltpu.VMEM((levels, rows, C), bf),
+            pltpu.VMEM((rows, C), bf),
+            dma((6,)), dma((6,)),
+            dma((2, levels)), dma((2, levels)),
             dma((3, n)), dma((3, n)),
-            dma((n,)), dma((n,)),
-            dma((2,)),
+            dma((3,)),
         ],
         compiler_params=pltpu.CompilerParams(collective_id=ident, has_side_effects=True),
     )(source, bank, weights)
@@ -215,9 +284,9 @@
 
 
 def block_kernel(
-    n, lat_ref, ws_ref, picked_ref, wt_ref, off_ref, out_ref,
-    qs, ks, vs, firsts, outgoing, hall, tproj, bias, tatt, back,
-    psend, precv, zsend, zrecv, bsend, brecv,
+    n, depth, lat_ref, sall_ref, picked_ref, part_ref, off_ref, out_ref,
+    ws_ref, wt_ref, tall, qs, ks, vs, firsts, outgoing, hall, tproj, bias, tatt, back,
+    psend, precv, zsend, zrecv, bsend, brecv, wsend, wrecv,
 ):
     me = lax.axis_index("frame")
     levels = n // PLANE
@@ -237,17 +306,14 @@
     for k in range(PLANE - 1):
         signal(mate(k))
 
-    @pl.when(has_up)
-    def _():
-        signal(me + PLANE)
-
-    @pl.when(has_down)
-    def _():
-        signal(me - PLANE)
-
-    pl.semaphore_wait(
-        barrier, PLANE - 1 + has_up.astype(jnp.int32) + has_down.astype(jnp.int32)
-    )
+    for k in range(1, levels):
+        signal(lax.rem(me + PLANE * k, n))
+    tall[me] = part_ref[...]
+    pl.semaphore_wait(barrier, PLANE - 1 + levels - 1)
+    relay = Relay(n, tall, wsend, wrecv)
+    relay.begin()
+    for i in range(n):
+        ws_ref[i * depth : (i + 1) * depth, :] = sall_ref[i, :depth, :]
 
     @pl.when(level == 0)
     def _():
@@ -327,10 +393,21 @@
             send_plane(f, k - 1).wait_recv()
             pass_on(f, k - 1)
 
+        @pl.when(t == 2)
+        def _():
+            relay.second()
+
+        @pl.when(t == 5)
+        def _():
+            relay.third()
+
         return carry
 
     lax.fori_loop(0, frames * PLANE, step, 0)
 
+    relay.arrive()
+    for i in range(n):
+        wt_ref[i * depth : (i + 1) * depth, :] = tall[i, :depth, :]
     time = PLANE * frames
     row = lax.broadcasted_iota(jnp.int32, bias.shape, 0)
     col = lax.broadcasted_iota(jnp.int32, bias.shape, 1)
@@ -416,6 +493,7 @@
             send_back(c, k).wait_recv()
         source = lax.rem(sub + PLANE - 1 - k, PLANE)
         finish(source, lambda f: back[source, f])
+    relay.drain()
     for k in range(last):
         for c in range(PIECES):
             send_back(c, k).wait_send()
@@ -432,7 +510,7 @@
                 send_level(f, k, False).wait_send()
 
 
-def block(latents, ws, picked, wt, offs, n, ident):
+def block(latents, sall, picked, part, offs, depth, n, ident):
     frames = latents.shape[0]
     spots = HW // PLANE
     time = PLANE * frames
@@ -440,11 +518,14 @@
     dma = pltpu.SemaphoreType.DMA
     bf = jnp.bfloat16
     return pl.pallas_call(
-        functools.partial(block_kernel, n),
+        functools.partial(block_kernel, n, depth),
         out_shape=jax.ShapeDtypeStruct(latents.shape, bf),
         in_specs=[vmem] * 4 + [pl.BlockSpec(memory_space=pltpu.SMEM)],
         out_specs=vmem,
         scratch_shapes=[
+            pltpu.VMEM((C, 4 * WIDE), bf),
+            pltpu.VMEM((C, 4 * WIDE), bf),
+            pltpu.VMEM((n,) + part.shape, bf),
             pltpu.VMEM((HW, WIDE), bf),
             pltpu.VMEM((2 * HW, WIDE), bf),
             pltpu.VMEM((2 * HW, WIDE), bf),
@@ -458,11 +539,12 @@
             dma((frames, PLANE)), dma((frames, PLANE)),
             dma((2, frames, PLANE)), dma((2, frames, PLANE)),
             dma((PIECES, PLANE)), dma((PIECES, PLANE)),
+            dma((3, n)), dma((3, n)),
         ],
         compiler_params=pltpu.CompilerParams(
             collective_id=ident, has_side_effects=True, vmem_limit_bytes=VMEM_LIMIT
         ),
-    )(latents, ws, picked, wt, offs)
+    )(latents, sall, picked, part, offs)
 
 
 def widen(weights):
@@ -480,7 +562,7 @@
     held = up16(depth + 1)
 
     packed_t = widen(jnp.concatenate([temporal_in, temporal_out.T], axis=1))
-    wt = lax.all_gather(packed_t, "frame", axis=0, tiled=True)
+    packed_t = jnp.pad(packed_t, ((0, up16(depth) - depth), (0, 0)))
 
     packed_s = widen(jnp.concatenate([spatial_in, spatial_out.T], axis=1))
     mark = jnp.broadcast_to(offsets.astype(jnp.bfloat16)[:, None], (1, 4 * WIDE))
@@ -488,10 +570,10 @@
         [packed_s, mark, jnp.zeros((held - depth - 1, 4 * WIDE), jnp.bfloat16)], axis=0
     )
     picked, gathered = collect(source_device, reference_bank, packed_s, n, 0)
-    ws = gathered[:, :depth].reshape(C, 4 * WIDE)
     level = lax.axis_index("frame") // PLANE
     offs = lax.dynamic_slice_in_dim(gathered[:, depth, 0], level * PLANE, PLANE, 0)
-    return block(latents, ws, picked.reshape(HW, C), wt, offs.astype(jnp.int32), n, 1)
+    picked = picked.reshape(HW, C)
+    return block(latents, gathered, picked, packed_t, offs.astype(jnp.int32), depth, n, 1)
 
 
 def solution(mesh):

time: 167 us -> 127 us (0.76)
  Pallas kernels: 141 us -> 117 us
  between operations: 14.8 us -> 1.37 us
  local copies, waits for them, and re-layouts: 7.61 us -> 4.7 us
    pallas_call x1, Pallas kernels: 66.1 us -> 45.4 us  [collect(): pl.pallas_call(functools.partial(collect_kernel, n, rows, holders), out_s...]
    pallas_call x1, Pallas kernels: 75.1 us -> 71.8 us  [block(): pl.pallas_call(functools.partial(block_kernel, n, depth), out_shape=jax.S...]
    slice x1 -> x0, local copies, waits for them, and re-layouts: 2.95 us -> none  [body(): ws = gathered[:, :depth].reshape(C, 4 * WIDE)]
  transfers between devices with their start and end apart: 1 -> 0, of which waited for: 0 -> 0; matrix products, arithmetic and copies ran while one was open for 4% -> 0% of each run, Pallas kernels for 40% -> 0%
where the time goes in v3:
time: 127 us
  Pallas kernels  117 us (92%)
  local copies, waits for them, and re-layouts  4.7 us (4%)
  other arithmetic  3.41 us (3%)
  between operations  1.37 us (1%)
    pallas_call x1, Pallas kernels, block(): pl.pallas_call(functools.partial(block_kernel, n, depth), out_shape=jax.S...  71.8 us
    pallas_call x1, Pallas kernels, collect(): pl.pallas_call(functools.partial(collect_kernel, n, rows, holders), out_s...  45.4 us
    unnamed x3, local copies, waits for them, and re-layouts  2.64 us

profile of v3, /device:TPU:0, one launch (start us, length us, event | category | flops | bytes accessed | tf_op | source)
XLA Modules:
  0.0 126.7 jit_solution(922439066891578657)
XLA Ops:
  1.3 0.1 pad.17.clone
  1.4 0.1 pad.18.clone
  1.5 1.0 pad_maximum_fusion
  2.4 0.2 reshape.21
  2.6 0.1 pad.11
  2.7 0.8 maximum_maximum_fusion.w_ref
  3.5 1.0 pad_maximum_fusion.1
  4.5 0.2 reshape.24
  4.6 0.1 pad.12
  4.7 0.7 pad.13.part_ref
  5.4 45.4 %shard_map.82 = (bf16[4,3,48,640]{3,2,1,0:T(8,128)(2,1)}, bf16[16,48,1536]{2,1,0:T(8,128)(2,1)}) custom-call(s32[1]{0:T(128)S(6)} %copy.13.src_ref, bf16[1,576,640]{2,1,0:T(8,128)(2,1)} %bank_ref.1, bf16[48,1536]{1,0:T(8,128)(2,1)} %maximum_maximum_fusion.w_ref), custom_call_target="tpu_custom_call" | custom-call | tf_op jit(solution)/shard_map/pallas_call | solution.py:241
  50.8 0.8 slice.3
  51.6 0.7 convert_reduce_fusion.off_ref
  52.3 71.8 %shard_map.83 = bf16[2,576,640]{2,1,0:T(8,128)(2,1)} custom-call(bf16[2,576,640]{2,1,0:T(8,128)(2,1)} %lat_ref.1, bf16[16,48,1536]{2,1,0:T(8,128)(2,1)} %get-tuple-element.7.sall_ref, bf16[576,640]{1,0:T(8,128)(2,1)} %bitcast.8, bf16[48,1536]{1,0:T(8,128)(2,1)} %pad.13.part_ref, s32[4]{0:T(128)} %convert_reduce_fusion.off_ref), custom_call_target="tpu_custom_call" | custom-call | tf_op jit(solution)/shard_map/pallas_call | solution.py:520
  124.1 2.6 %copy.14 = bf16[2,576,640]{2,1,0:T(8,128)(2,1)} copy(bf16[2,576,640]{2,1,0:T(8,128)(2,1)} %shard_map.83) | data formatting | bytes 2949120
  (3 shorter events, 0.0 us)

commit v4 on v3

--- a/solution.py
+++ b/solution.py
@@ -61,7 +61,8 @@
 
 
 class Relay:
-    def __init__(self, n, wall, send, recv):
+    def __init__(self, n, wall, send, recv, along=True):
+        self.first = 1 if along else n
         self.n, self.levels = n, n // PLANE
         self.wall, self.send, self.recv = wall, send, recv
         self.me = lax.axis_index("frame")
@@ -81,14 +82,15 @@
         )
 
     def begin(self):
-        for k in range(1, self.levels):
+        for k in range(self.first, self.levels):
             self.along(k).start()
         self.hop(1, self.me, 0, 0).start()
         self.hop(2, self.me, 0, 0).start()
 
     def second(self):
         for k in range(1, self.levels):
-            self.along(k).wait_recv()
+            if k >= self.first:
+                self.along(k).wait_recv()
             self.hop(1, self.me, k, k).start()
             self.hop(2, self.me, k, k).start()
 
@@ -104,7 +106,7 @@
 
     def drain(self):
         for k in range(self.levels):
-            if k:
+            if k >= self.first:
                 self.along(k).wait_send()
             self.hop(1, self.me, k, k).wait_send()
             self.hop(2, self.me, k, k).wait_send()
@@ -112,8 +114,8 @@
 
 
 def collect_kernel(
-    n, rows, holders, src_ref, bank_ref, w_ref, ref_ref, wall_ref,
-    pair, cross, out_x, out_z, got, chunk, csend, crecv, zsend, zrecv, wsend, wrecv, local,
+    n, rows, holders, src_ref, bank_ref, w_ref, t_ref, ref_ref, wall_ref, line_ref,
+    pair, cross, out_x, out_z, got, chunk, csend, crecv, zsend, zrecv, wsend, wrecv, tsend, trecv, local,
 ):
     me = lax.axis_index("frame")
     sub, level = lax.rem(me, PLANE), me // PLANE
@@ -127,6 +129,19 @@
         pl.semaphore_signal(barrier, inc=1, device_id={"frame": peer}, device_id_type=MESH)
     place = pltpu.make_async_copy(w_ref, wall_ref.at[me], local.at[0])
     place.start()
+    keep = pltpu.make_async_copy(t_ref, line_ref.at[level], local.at[3])
+    keep.start()
+
+    def line(k):
+        return remote(
+            t_ref, line_ref.at[level], tsend.at[k], trecv.at[k], lax.rem(me + PLANE * k, n)
+        )
+
+    def line_from(k):
+        return remote(
+            t_ref, line_ref.at[lax.rem(level + levels - k, levels)], tsend.at[k], trecv.at[k],
+            lax.rem(me + PLANE * k, n),
+        )
 
     def bank_rows(x, c):
         start = pl.multiple_of((2 * x + c) * spots, 16)
@@ -199,6 +214,8 @@
         def _():
             gather(k, sender).wait_recv()
 
+    for k in range(1, levels):
+        line(k).start()
     other = lax.rem(sub + 2, PLANE)
 
     def plane_copy(which, slot, peer):
@@ -215,6 +232,10 @@
     plane_copy(lax.rem(cmate, PLANE), 4, cmate).wait_recv()
     plane_copy(lax.rem(across(cmate), PLANE), 5, cmate).wait_recv()
     relay.drain()
+    keep.wait()
+    for k in range(1, levels):
+        line_from(k).wait_recv()
+        line(k).wait_send()
     for x in range(2):
         core_copy(x).wait_send()
     x_copy.wait_send()
@@ -231,7 +252,7 @@
             gather(k, level).wait_send()
 
 
-def collect(source, bank, weights, n, ident):
+def collect(source, bank, weights, later, n, ident):
     spots, levels = HW // PLANE, n // PLANE
     rows = up16(-(-spots // levels))
     holders = spots // rows
@@ -243,9 +264,10 @@
         out_shape=(
             jax.ShapeDtypeStruct((PLANE, holders, rows, C), bf),
             jax.ShapeDtypeStruct((n,) + weights.shape, bf),
+            jax.ShapeDtypeStruct((levels,) + later.shape, bf),
         ),
-        in_specs=[pl.BlockSpec(memory_space=pltpu.SMEM), any_spec, any_spec],
-        out_specs=(any_spec, any_spec),
+        in_specs=[pl.BlockSpec(memory_space=pltpu.SMEM), any_spec, any_spec, any_spec],
+        out_specs=(any_spec, any_spec, any_spec),
         scratch_shapes=[
             pltpu.VMEM((2, 2, spots, C), bf),
             pltpu.VMEM((2, spots, C), bf),
@@ -256,10 +278,11 @@
             dma((6,)), dma((6,)),
             dma((2, levels)), dma((2, levels)),
             dma((3, n)), dma((3, n)),
-            dma((3,)),
+            dma((levels,)), dma((levels,)),
+            dma((4,)),
         ],
         compiler_params=pltpu.CompilerParams(collective_id=ident, has_side_effects=True),
-    )(source, bank, weights)
+    )(source, bank, weights, later)
 
 
 def heads_of(queries, keys, values, bias):
@@ -283,6 +306,17 @@
     return jnp.concatenate(blocks, axis=1).astype(jnp.bfloat16)
 
 
+def unfold(n, depth, wall, wide):
+    for j in range(4):
+        wide[:, j * WIDE + INNER : (j + 1) * WIDE] = jnp.zeros(
+            (n * depth, WIDE - INNER), jnp.bfloat16
+        )
+        for i in range(n):
+            wide[i * depth : (i + 1) * depth, j * WIDE : j * WIDE + INNER] = wall[
+                i, :depth, j * INNER : (j + 1) * INNER
+            ]
+
+
 def block_kernel(
     n, depth, lat_ref, sall_ref, picked_ref, part_ref, off_ref, out_ref,
     ws_ref, wt_ref, tall, qs, ks, vs, firsts, outgoing, hall, tproj, bias, tatt, back,
@@ -308,12 +342,13 @@
 
     for k in range(1, levels):
         signal(lax.rem(me + PLANE * k, n))
-    tall[me] = part_ref[...]
+    for i in range(levels):
+        tall[PLANE * i + sub] = part_ref[i]
     pl.semaphore_wait(barrier, PLANE - 1 + levels - 1)
-    relay = Relay(n, tall, wsend, wrecv)
+    relay = Relay(n, tall, wsend, wrecv, along=False)
     relay.begin()
-    for i in range(n):
-        ws_ref[i * depth : (i + 1) * depth, :] = sall_ref[i, :depth, :]
+    relay.second()
+    unfold(n, depth, sall_ref, ws_ref)
 
     @pl.when(level == 0)
     def _():
@@ -393,11 +428,7 @@
             send_plane(f, k - 1).wait_recv()
             pass_on(f, k - 1)
 
-        @pl.when(t == 2)
-        def _():
-            relay.second()
-
-        @pl.when(t == 5)
+        @pl.when(t == 3)
         def _():
             relay.third()
 
@@ -406,8 +437,7 @@
     lax.fori_loop(0, frames * PLANE, step, 0)
 
     relay.arrive()
-    for i in range(n):
-        wt_ref[i * depth : (i + 1) * depth, :] = tall[i, :depth, :]
+    unfold(n, depth, tall, wt_ref)
     time = PLANE * frames
     row = lax.broadcasted_iota(jnp.int32, bias.shape, 0)
     col = lax.broadcasted_iota(jnp.int32, bias.shape, 1)
@@ -525,7 +555,7 @@
         scratch_shapes=[
             pltpu.VMEM((C, 4 * WIDE), bf),
             pltpu.VMEM((C, 4 * WIDE), bf),
-            pltpu.VMEM((n,) + part.shape, bf),
+            pltpu.VMEM((n,) + part.shape[1:], bf),
             pltpu.VMEM((HW, WIDE), bf),
             pltpu.VMEM((2 * HW, WIDE), bf),
             pltpu.VMEM((2 * HW, WIDE), bf),
@@ -547,12 +577,6 @@
     )(latents, sall, picked, part, offs)
 
 
-def widen(weights):
-    parts = weights.reshape(weights.shape[0], 4, INNER)
-    parts = jnp.pad(parts, ((0, 0), (0, 0), (0, WIDE - INNER)))
-    return parts.reshape(weights.shape[0], 4 * WIDE)
-
-
 def body(
     latents, offsets, source_device, reference_bank,
     spatial_in, spatial_out, temporal_in, temporal_out,
@@ -561,19 +585,21 @@
     depth = spatial_in.shape[0]
     held = up16(depth + 1)
 
-    packed_t = widen(jnp.concatenate([temporal_in, temporal_out.T], axis=1))
+    packed_t = jnp.concatenate([temporal_in, temporal_out.T], axis=1)
     packed_t = jnp.pad(packed_t, ((0, up16(depth) - depth), (0, 0)))
 
-    packed_s = widen(jnp.concatenate([spatial_in, spatial_out.T], axis=1))
-    mark = jnp.broadcast_to(offsets.astype(jnp.bfloat16)[:, None], (1, 4 * WIDE))
+    packed_s = jnp.concatenate([spatial_in, spatial_out.T], axis=1)
+    mark = jnp.broadcast_to(offsets.astype(jnp.bfloat16)[:, None], (1, 4 * INNER))
     packed_s = jnp.concatenate(
-        [packed_s, mark, jnp.zeros((held - depth - 1, 4 * WIDE), jnp.bfloat16)], axis=0
+        [packed_s, mark, jnp.zeros((held - depth - 1, 4 * INNER), jnp.bfloat16)], axis=0
     )
-    picked, gathered = collect(source_device, reference_bank, packed_s, n, 0)
+    picked, gathered, lines = collect(
+        source_device, reference_bank, packed_s, packed_t, n, 0
+    )
     level = lax.axis_index("frame") // PLANE
     offs = lax.dynamic_slice_in_dim(gathered[:, depth, 0], level * PLANE, PLANE, 0)
     picked = picked.reshape(HW, C)
-    return block(latents, gathered, picked, packed_t, offs.astype(jnp.int32), depth, n, 1)
+    return block(latents, gathered, picked, lines, offs.astype(jnp.int32), depth, n, 1)
 
 
 def solution(mesh):

time: 127 us -> 124 us (0.976)
    pallas_call x1, Pallas kernels: 45.4 us -> 41.4 us  [collect(): pl.pallas_call(functools.partial(collect_kernel, n, rows, holders), out_s...]
    pallas_call x1, Pallas kernels: 71.8 us -> 75 us  [block(): pl.pallas_call(functools.partial(block_kernel, n, depth), out_shape=jax.S...]
    concatenate x3 -> x1, other arithmetic: 2.73 us -> 1.75 us  [body(): packed_t = jnp.concatenate([temporal_in, temporal_out.T], axis=1)]
    unnamed x3 -> x1, local copies, waits for them, and re-layouts: 2.64 us -> 2.61 us
where the time goes in v4:
time: 124 us
  Pallas kernels  116 us (94%)
  local copies, waits for them, and re-layouts  3.53 us (3%)
  other arithmetic  2.43 us (2%)
  between operations  1.32 us (1%)
    pallas_call x1, Pallas kernels, block(): pl.pallas_call(functools.partial(block_kernel, n, depth), out_shape=jax.S...  75 us
    pallas_call x1, Pallas kernels, collect(): pl.pallas_call(functools.partial(collect_kernel, n, rows, holders), out_s...  41.4 us
    unnamed x1, local copies, waits for them, and re-layouts  2.61 us

profile of v4, /device:TPU:0, one launch (start us, length us, event | category | flops | bytes accessed | tf_op | source)
XLA Modules:
  0.0 123.7 jit_solution(12842083499500473738)
XLA Ops:
  1.3 0.1 pad.8.clone
  1.4 0.1 pad.9.clone
  1.5 1.8 %fusion.2 = (bf16[48,1280]{1,0:T(8,128)(2,1)}, bf16[48,1280]{1,0:T(8,128)(2,1)}) fusion(bf16[40,320]{1,0:T(8,128)(2,1)} %bitcast.5, bf16[40,960]{1,0:T(8,128)(2,1)} %param.14, bf16[48]{0:T(256)(128)(2,1)S(1)} %pad.9.clone, bf16[48]{0:T(256)(128)(2,1)S(1)} %pad.8.clone, bf16[40,320]{1,0:T(8,128)(2,1)} %bitcast.6, bf16[40,960]{1,0:T(8,128)(2,1)} %param.12), kind=kLoop, calls=%fused_computation.3 | loop fusion | flops 921600 | bytes 450752 | tf_op jit(solution)/shard_map/concatenate | solution.py:588
  3.2 41.4 %shard_map.82 = (bf16[4,3,48,640]{3,2,1,0:T(8,128)(2,1)}, bf16[16,48,1280]{2,1,0:T(8,128)(2,1)}, bf16[4,48,1280]{2,1,0:T(8,128)(2,1)}) custom-call(s32[1]{0:T(128)S(6)} %copy.11.src_ref, bf16[1,576,640]{2,1,0:T(8,128)(2,1)} %bank_ref.1, bf16[48,1280]{1,0:T(8,128)(2,1)} %get-tuple-element.12.w_ref, bf16[48,1280]{1,0:T(8,128)(2,1)} %get-tuple-element.11.t_ref), custom_call_target="tpu_custom_call" | custom-call | tf_op jit(solution)/shard_map/pallas_call | solution.py:262
  44.7 0.8 slice.3
  45.4 0.7 convert_reduce_fusion.off_ref
  46.1 75.0 %shard_map.83 = bf16[2,576,640]{2,1,0:T(8,128)(2,1)} custom-call(bf16[2,576,640]{2,1,0:T(8,128)(2,1)} %lat_ref.1, bf16[16,48,1280]{2,1,0:T(8,128)(2,1)} %get-tuple-element.8.sall_ref, bf16[576,640]{1,0:T(8,128)(2,1)} %bitcast.4, bf16[4,48,1280]{2,1,0:T(8,128)(2,1)} %get-tuple-element.10.part_ref, s32[4]{0:T(128)} %convert_reduce_fusion.off_ref), custom_call_target="tpu_custom_call" | custom-call | tf_op jit(solution)/shard_map/pallas_call | solution.py:550
  121.1 2.6 %copy.12 = bf16[2,576,640]{2,1,0:T(8,128)(2,1)} copy(bf16[2,576,640]{2,1,0:T(8,128)(2,1)} %shard_map.83) | data formatting | bytes 2949120
  (1 shorter events, 0.0 us)
